TPU v7x, 32 devices: a whole 2x2x4 slice. The times are simulated.
32 devices in a mesh: slab: 16 (over z, y, core), blk: 2 (over x).
Axes of the slice: x: 2, y: 2, z: 4, core: 2. Of those that a mesh axis runs over, the one named last changes fastest.
Arguments:
- residual: bfloat16 [16, 16, 8, 40, 128], P('slab', 'blk'), may hold values from -6 to 6
- tile_values: bfloat16 [16, 2, 5, 64, 128, 128], P('slab', 'blk'), may hold values from -0.109375 to 0.109375
- row_index: int32 [16, 2, 5, 64], P('slab', 'blk'), may hold values from 0 to 15
- voxel_index: int32 [16, 2, 5, 64], P('slab', 'blk'), may hold values from 0 to 255
- slot_count: int32 [16, 2, 5], P('slab', 'blk'), may hold values from 8 to 64, as said below
- tof_shift: int32 [40], replicated, may hold values from -20 to 19, as said below
Outputs:
- gradient_image: float32 [16, 512, 8, 128], P('slab', 'blk')
Inputs may be any that keep to these rules, and one draw needn't show every extreme that they name: `slot_count`: slots at or beyond a list's count are unused; some list is full in every draw. `tof_shift`: every TOF bin has its own offset: the 40 offsets are the whole numbers of the range, each once, in an order drawn from the seed.
All inputs are finite; a program needn't handle non-finite values.
Results may differ from a plain program's by a relative error of at most 0.0003.
Values may be sent and summed in bfloat16 or wider, within the bound.
A program may use at most 128 MiB of HBM per device.

v0:
```python
from functools import partial

import jax
import jax.numpy as jnp
from jax import lax
from jax.experimental import pallas as pl
from jax.experimental.pallas import tpu as pltpu
from jax.sharding import PartitionSpec as P

VT = 256
UNROLL = 4
CHUNKS = 4
GROUP = 64
TOP = 32767.0
STEPS = 8.0
LIMIT = 50 * 1024 * 1024
SMEM = pl.BlockSpec(memory_space=pltpu.SMEM)
VMEM = pl.BlockSpec(memory_space=pltpu.VMEM)
HBM = pl.BlockSpec(memory_space=pl.ANY)

FAR, IN2, IN1, NEAR, OWN = range(5)


def sort_kernel(shift_ref, res_ref, out_ref, *, gates, bins):
    size = gates * bins
    dst = lax.broadcasted_iota(jnp.int32, (size, size), 0)
    src = lax.broadcasted_iota(jnp.int32, (size, size), 1)
    pick = ((shift_ref[...] + bins // 2) == dst // gates) & (src // bins == dst % gates)
    mat = pick.astype(jnp.float32).astype(jnp.bfloat16)
    for i in range(res_ref.shape[0]):
        out_ref[i] = jnp.dot(mat, res_ref[i], preferred_element_type=jnp.float32).astype(jnp.bfloat16)


def sort_rows(shift_row, res):
    count, gates, bins, depth = res.shape
    size = gates * bins
    return pl.pallas_call(
        partial(sort_kernel, gates=gates, bins=bins),
        out_shape=jax.ShapeDtypeStruct((count, size, depth), jnp.bfloat16),
        in_specs=[VMEM, VMEM],
        out_specs=VMEM,
        compiler_params=pltpu.CompilerParams(vmem_limit_bytes=LIMIT),
        cost_estimate=pl.CostEstimate(
            flops=2 * count * size * size * depth, bytes_accessed=4_000_000, transcendentals=0
        ),
    )(shift_row, res.reshape(count, size, depth))


def add_slots(acc, buf, sino, slot_of, row_of, voxel_of, total, gates, bins):
    size = gates * bins
    dump = VT + bins

    def group(i, carry):
        first = i * UNROLL
        outs = []
        ats = []
        for u in range(UNROLL):
            k = first + u
            live = k < total
            j = jnp.where(live, slot_of(k), 0)
            row = jnp.where(live, row_of(k, j), 0)
            v = jnp.where(live, voxel_of(j), dump)
            ats.append(pl.ds(pl.multiple_of(v * gates, gates), size))
            outs.append(jnp.dot(sino[row], buf[j], preferred_element_type=jnp.float32))
        for at, out in zip(ats, outs):
            acc[at] += out
        return carry

    lax.fori_loop(0, (total + UNROLL - 1) // UNROLL, group, 0)


def first_kernel(meta, rows, voxels, sino, tiles, *rest, gates, bins, slots, local_rows):
    *parts, far_slots, far_rows, far_counts, acc, buf, near_slots, sems = rest
    lists = len(parts)
    per = slots // CHUNKS
    lead = bins // 2 * gates
    span = VT * gates
    block, blocks = meta[2 * lists], meta[2 * lists + 1]

    def chunk_copy(r, c):
        return pltpu.make_async_copy(
            tiles.at[meta[r], pl.ds(c * per, per)], buf.at[r, pl.ds(c * per, per)], sems.at[r, c]
        )

    for r in range(lists):
        for c in range(CHUNKS):
            @pl.when(c * per < meta[lists + r])
            def _():
                chunk_copy(r, c).start()

    for r in range(lists):
        which, count = meta[r], meta[lists + r]

        def split(j, found):
            here, there = found
            row = rows[which, j]
            owner = row // local_rows
            mine = owner == block
            hop = block - owner
            hop = jnp.where(hop < 0, hop + blocks, hop)
            near_slots[here] = j
            far_slots[r, there] = j
            far_rows[r, there] = (hop - 1) * local_rows + row % local_rows
            step = mine.astype(jnp.int32)
            return here + step, there + 1 - step

        here, there = lax.fori_loop(0, count, split, (0, 0))
        far_counts[r] = there
        acc[...] = jnp.zeros(acc.shape, jnp.float32)
        for c in range(CHUNKS):
            @pl.when(c * per < count)
            def _():
                chunk_copy(r, c).wait()
        add_slots(
            acc, buf.at[r], sino, lambda k: near_slots[k],
            lambda k, j: rows[which, j] % local_rows, lambda j: voxels[which, j],
            here, gates, bins,
        )
        parts[r][...] = acc[lead:lead + span]


def rest_kernel(
    meta, far_slots, far_rows, far_counts, voxels, sino, tiles, init, *rest,
    role, gates, bins, slots, send, lists
):
    rest = list(rest)
    got = rest.pop(0) if role in (NEAR, OWN) else None
    out, acc, buf, sems = rest
    which, count = meta[role], meta[lists + role]
    per = slots // CHUNKS
    lead = bins // 2 * gates
    span = VT * gates

    def chunk_copy(c):
        return pltpu.make_async_copy(
            tiles.at[which, pl.ds(c * per, per)], buf.at[pl.ds(c * per, per)], sems.at[c]
        )

    for c in range(CHUNKS):
        @pl.when(c * per < count)
        def _():
            chunk_copy(c).start()

    acc[0:lead] = jnp.zeros((lead, acc.shape[1]), jnp.float32)
    acc[lead + span:] = jnp.zeros((acc.shape[0] - lead - span, acc.shape[1]), jnp.float32)
    if got is None:
        acc[lead:lead + span] = init[...]
    else:
        acc[lead:lead + span] = init[...] + got[...]
    for c in range(CHUNKS):
        @pl.when(c * per < count)
        def _():
            chunk_copy(c).wait()
    add_slots(
        acc, buf, sino, lambda k: far_slots[role, k], lambda k, j: far_rows[role, k],
        lambda j: voxels[which, j], far_counts[role], gates, bins,
    )
    if send:
        groups = span // GROUP
        vals = acc[lead:lead + span].reshape(groups, GROUP, acc.shape[1])
        top = jnp.maximum(jnp.max(jnp.abs(vals), axis=1), 1e-30)
        code = jnp.ceil(STEPS * jnp.log2(top))
        inv = TOP * jnp.exp2(code * (-1.0 / STEPS))
        q = jnp.clip(jnp.round(vals * inv[:, None, :]), -TOP, TOP)
        out[0:span] = q.astype(jnp.int32).astype(jnp.int16).reshape(span, acc.shape[1])
        out[span:] = code.astype(jnp.int32).astype(jnp.int16)
    else:
        out[...] = acc[lead:lead + span]


def local(residual, tile_values, row_index, voxel_index, slot_count, tof_shift):
    local_rows, gates, bins, depth = residual.shape[1:]
    lists, slots, _, width = tile_values.shape[2:]
    size = gates * bins
    span = VT * gates
    tiles = tile_values[0, 0]
    rows = row_index[0, 0]
    voxels = voxel_index[0, 0]
    counts = slot_count[0, 0]
    slabs = lax.axis_size("slab")
    blocks = lax.axis_size("blk")
    res = residual[0]
    others = [
        lax.ppermute(res, "blk", [(i, (i + hop) % blocks) for i in range(blocks)])
        for hop in range(1, blocks)
    ]

    sign = 2 * lax.rem(lax.axis_index("slab"), 2) - 1
    order = 2 + sign * jnp.array([2, -2, -1, 1, 0], jnp.int32)
    lived = jnp.sum(jnp.where(order[:, None] == jnp.arange(lists)[None, :], counts[None, :], 0), axis=1)
    place = jnp.stack([lax.axis_index("blk"), blocks]).astype(jnp.int32)
    meta = jnp.concatenate([order, lived.astype(jnp.int32), place])

    shift_row = jnp.tile(tof_shift, gates).reshape(1, size)
    acc = pltpu.VMEM((span + bins * gates + size, width), jnp.float32)
    image = jax.ShapeDtypeStruct((span, width), jnp.float32)
    table = jax.ShapeDtypeStruct((lists, slots), jnp.int32)
    *parts, far_slots, far_rows, far_counts = pl.pallas_call(
        partial(first_kernel, gates=gates, bins=bins, slots=slots, local_rows=local_rows),
        out_shape=[image] * lists + [table, table, jax.ShapeDtypeStruct((lists,), jnp.int32)],
        in_specs=[SMEM, SMEM, SMEM, VMEM, HBM],
        out_specs=[VMEM] * lists + [SMEM] * 3,
        scratch_shapes=[
            acc,
            pltpu.VMEM((lists, slots, depth, width), jnp.bfloat16),
            pltpu.SMEM((slots,), jnp.int32),
            pltpu.SemaphoreType.DMA((lists, CHUNKS)),
        ],
        compiler_params=pltpu.CompilerParams(vmem_limit_bytes=LIMIT),
        cost_estimate=pl.CostEstimate(
            flops=4 * lists * slots * size * depth * width, bytes_accessed=20_000_000, transcendentals=0
        ),
    )(meta, rows, voxels, sort_rows(shift_row, res), tiles)

    sino = sort_rows(shift_row, others[0] if len(others) == 1 else jnp.concatenate(others))

    def run(role, after, got=None):
        send = role in (FAR, NEAR)
        if after is not None:
            held, after = lax.optimization_barrier((meta, after))
        else:
            held = meta
        extra = [] if got is None else [got]
        shape = jax.ShapeDtypeStruct((span + span // GROUP, width), jnp.int16) if send else image
        out = pl.pallas_call(
            partial(
                rest_kernel, role=role, gates=gates, bins=bins, slots=slots, send=send, lists=lists
            ),
            out_shape=shape,
            in_specs=[SMEM] * 5 + [VMEM, HBM, VMEM] + [VMEM] * len(extra),
            out_specs=VMEM,
            scratch_shapes=[
                acc,
                pltpu.VMEM((slots, depth, width), jnp.bfloat16),
                pltpu.SemaphoreType.DMA((CHUNKS,)),
            ],
            compiler_params=pltpu.CompilerParams(vmem_limit_bytes=LIMIT),
            cost_estimate=pl.CostEstimate(
                flops=2 * slots * size * depth * width, bytes_accessed=6_000_000, transcendentals=0
            ),
        )(held, far_slots, far_rows, far_counts, voxels, sino, tiles, parts[role], *extra)
        return out, after

    mate = [(i, i ^ 1) for i in range(slabs)]

    def outward(distance):
        route = []
        for i in range(slabs):
            j = i + (distance if i % 2 else -distance)
            if 0 <= j < slabs:
                route.append((i, j))
        return route

    far, _ = run(FAR, None)
    in2, far = run(IN2, far)
    far = lax.ppermute(far, "slab", outward(2))
    in1, in2 = run(IN1, in2)
    in2 = lax.ppermute(in2, "slab", mate)
    near, in1 = run(NEAR, in1, in2)
    in1 = lax.ppermute(in1, "slab", mate)
    own, near = run(OWN, near, in1)
    near = lax.ppermute(near, "slab", outward(1))

    def widen(sent):
        scale = jnp.exp2(sent[span:].astype(jnp.float32) * (1.0 / STEPS)) * (1.0 / TOP)
        values = sent[:span].astype(jnp.float32).reshape(span // GROUP, GROUP, width)
        return (values * scale[:, None, :]).reshape(span, width)

    image_sum = own + widen(far) + widen(near)
    return image_sum.reshape(1, VT, gates, width)


def solution(mesh):
    placed = (
        P("slab", "blk", None, None, None),
        P("slab", "blk", None, None, None, None),
        P("slab", "blk", None, None),
        P("slab", "blk", None, None),
        P("slab", "blk", None),
        P(),
    )
    return jax.shard_map(
        local, mesh=mesh, in_specs=placed, out_specs=P("slab", "blk", None, None), check_vma=False
    )
```

profile of v0, /device:TPU:11, one launch (start us, length us, event | category | flops | bytes accessed | tf_op | source)
XLA Modules:
  0.0 66.1 jit_solution(15549761460266584450)
XLA Ops:
  0.0 0.3 collective-permute-start
  0.3 0.7 multiply_add_fusion
  0.9 0.8 %select_reduce_fusion = s32[5]{0:T(128)S(1)} fusion(s32[5]{0:T(128)} %bitcast.39, s32[5]{0:T(128)S(1)} %multiply_add_fusion), kind=kLoop, calls=%fused_computation.8 | loop fusion | flops 70 | bytes 60 | tf_op jit(solution)/shard_map/reduce_sum | solution.py:190
  1.8 0.1 pad_add_fusion.meta
  1.8 0.7 %copy.12 = s32[1,1,5,64]{3,2,1,0:T(8,128)S(1)} copy(s32[1,1,5,64]{3,1,2,0:T(1,128)} %param.10) | data formatting | bytes 2560
  2.5 0.7 tile.2
  3.2 0.1 reshape_tile.3.shift_ref
  3.3 0.7 %copy.13 = s32[1,1,5,64]{3,2,1,0:T(8,128)S(1)} copy(s32[1,1,5,64]{3,1,2,0:T(1,128)} %param.9) | data formatting | bytes 2560
  3.9 0.0 copy-start.2
  3.9 1.1 %copy-done.2 = bf16[1,8,8,40,128]{4,3,2,1,0:T(8,128)(2,1)S(1)} copy-done((bf16[1,8,8,40,128]{4,3,2,1,0:T(8,128)(2,1)S(1)}, bf16[1,8,8,40,128]{4,3,2,1,0:T(8,128)(2,1)}, u32[]{:S(2)}) %copy-start.2) | copy-done | bytes 655384
  5.0 0.7 %shard_map.73.sino = bf16[8,320,128]{2,1,0:T(8,128)(2,1)S(1)} custom-call(s32[1,320]{1,0:T(1,128)S(1)} %reshape_tile.3.shift_ref, bf16[8,320,128]{2,1,0:T(8,128)(2,1)S(1)} %bitcast.24), custom_call_target="tpu_custom_call" | custom-call | flops 209715200 | bytes 4000000 | tf_op jit(solution)/shard_map/pallas_call | solution.py:37
  5.7 17.0 %shard_map.74 = (f32[2048,128]{1,0:T(8,128)S(1)}, f32[2048,128]{1,0:T(8,128)S(1)}, f32[2048,128]{1,0:T(8,128)S(1)}, f32[2048,128]{1,0:T(8,128)}, f32[2048,128]{1...) custom-call(s32[12]{0:T(128)S(1)} %pad_add_fusion.meta, s32[5,64]{1,0:T(8,128)S(1)} %bitcast.32, ...), custom_call_target="tpu_custom_call" | custom-call | flops 6710886400 | bytes 20000000 | tf_op jit(solution)/shard_map/pallas_call | solution.py:198
  22.7 0.0 collective-permute-done
  22.8 0.7 %shard_map.75.sino = bf16[8,320,128]{2,1,0:T(8,128)(2,1)S(1)} custom-call(s32[1,320]{1,0:T(1,128)S(1)} %reshape_tile.3.shift_ref, bf16[8,320,128]{2,1,0:T(8,128)(2,1)S(1)} %bitcast.25), custom_call_target="tpu_custom_call" | custom-call | flops 209715200 | bytes 4000000 | tf_op jit(solution)/shard_map/pallas_call | solution.py:37
  23.4 4.1 %shard_map.76 = s16[2080,128]{1,0:T(8,128)(2,1)S(1)} custom-call(s32[12]{0:T(128)S(1)} %pad_add_fusion.meta, s32[5,64]{1,0:T(8,128)S(1)} %get-tuple-element.21.far_slots, s32[5,64]{1,0:T(8,128)S(1)} %get-tuple-element.22.far_rows, s32[5]{0:T(128)S(1)} %get-tuple-element.23.far_counts, s32[5,64]{1,0:T(8,128)S(1)} %bitcast.27, ...), custom_call_target="tpu_custom_call" | custom-call | flops 671088640 | bytes 6000000 | tf_op jit(solution)/shard_map/pallas_call | solution.py:225
  27.5 0.0 copy-start
  27.5 3.9 %shard_map.77 = f32[2048,128]{1,0:T(8,128)S(1)} custom-call(s32[12]{0:T(128)S(1)} %pad_add_fusion.meta, s32[5,64]{1,0:T(8,128)S(1)} %get-tuple-element.21.far_slots, s32[5,64]{1,0:T(8,128)S(1)} %get-tuple-element.22.far_rows, s32[5]{0:T(128)S(1)} %get-tuple-element.23.far_counts, s32[5,64]{1,0:T(8,128)S(1)} %bitcast.28, ...), custom_call_target="tpu_custom_call" | custom-call | flops 671088640 | bytes 6000000 | tf_op jit(solution)/shard_map/pallas_call | solution.py:225
  31.4 0.1 collective-permute-start.1
  31.5 0.0 copy-start.1
  31.5 5.1 %shard_map.78 = f32[2048,128]{1,0:T(8,128)S(1)} custom-call(s32[12]{0:T(128)S(1)} %pad_add_fusion.meta, s32[5,64]{1,0:T(8,128)S(1)} %get-tuple-element.21.far_slots, s32[5,64]{1,0:T(8,128)S(1)} %get-tuple-element.22.far_rows, s32[5]{0:T(128)S(1)} %get-tuple-element.23.far_counts, s32[5,64]{1,0:T(8,128)S(1)} %bitcast.29, ...), custom_call_target="tpu_custom_call" | custom-call | flops 671088640 | bytes 6000000 | tf_op jit(solution)/shard_map/pallas_call | solution.py:225
  36.6 0.1 collective-permute-start.2
  36.7 1.9 %collective-permute-start.3 = (s16[2080,128]{1,0:T(8,128)(2,1)S(1)}, s16[2080,128]{1,0:T(8,128)(2,1)S(1)}, u32[]{:S(2)}, u32[]{:S(2)}) collective-permute-start(s16[2080,128]{1,0:T(8,128)(2,1)S(1)} %shard_map.76), channel_id=1, source_target_pairs={{2,6},{4,0},{6,10},{8,4},{10,14},{12,8},{14,18},{16,12},{18,22},{2... | collective-permute-start | bytes 1597448 | tf_op jit(solution)/shard_map/ppermute | solution.py:256
  38.6 0.0 collective-permute-done.1.rest_0_
  38.6 0.0 copy-done
  38.7 3.2 %shard_map.79 = s16[2080,128]{1,0:T(8,128)(2,1)S(1)} custom-call(s32[12]{0:T(128)S(1)} %pad_add_fusion.meta, s32[5,64]{1,0:T(8,128)S(1)} %get-tuple-element.21.far_slots, s32[5,64]{1,0:T(8,128)S(1)} %get-tuple-element.22.far_rows, s32[5]{0:T(128)S(1)} %get-tuple-element.23.far_counts, s32[5,64]{1,0:T(8,128)S(1)} %bitcast.30, ...), custom_call_target="tpu_custom_call" | custom-call | flops 671088640 | bytes 6000000 | tf_op jit(solution)/shard_map/pallas_call | solution.py:225
  41.9 3.8 %collective-permute-start.4 = (s16[2080,128]{1,0:T(8,128)(2,1)S(1)}, s16[2080,128]{1,0:T(8,128)(2,1)S(1)}, u32[]{:S(2)}, u32[]{:S(2)}) collective-permute-start(s16[2080,128]{1,0:T(8,128)(2,1)S(1)} %shard_map.79), channel_id=1, source_target_pairs={{2,4},{4,2},{6,8},{8,6},{10,12},{12,10},{14,16},{16,14},{18,20},{2... | collective-permute-start | bytes 1597448 | tf_op jit(solution)/shard_map/ppermute | solution.py:262
  45.7 8.4 %collective-permute-done.3 = s16[2080,128]{1,0:T(8,128)(2,1)S(1)} collective-permute-done((s16[2080,128]{1,0:T(8,128)(2,1)S(1)}, s16[2080,128]{1,0:T(8,128)(2,1)S(1)}, u32[]{:S(2)}, u32[]{:S(2)}) %collective-permute-start.3) | collective-permute-done | bytes 532512 | tf_op jit(solution)/shard_map/ppermute | solution.py:256
  54.1 0.0 collective-permute-done.2.rest_0_
  54.1 0.0 copy-done.1
  54.1 4.6 %shard_map.80 = f32[2048,128]{1,0:T(8,128)S(1)} custom-call(s32[12]{0:T(128)S(1)} %pad_add_fusion.meta, s32[5,64]{1,0:T(8,128)S(1)} %get-tuple-element.21.far_slots, s32[5,64]{1,0:T(8,128)S(1)} %get-tuple-element.22.far_rows, s32[5]{0:T(128)S(1)} %get-tuple-element.23.far_counts, s32[5,64]{1,0:T(8,128)S(1)} %bitcast.31, ...), custom_call_target="tpu_custom_call" | custom-call | flops 671088640 | bytes 6000000 | tf_op jit(solution)/shard_map/pallas_call | solution.py:225
  58.8 6.0 %collective-permute-done.4 = s16[2080,128]{1,0:T(8,128)(2,1)S(1)} collective-permute-done((s16[2080,128]{1,0:T(8,128)(2,1)S(1)}, s16[2080,128]{1,0:T(8,128)(2,1)S(1)}, u32[]{:S(2)}, u32[]{:S(2)}) %collective-permute-start.4) | collective-permute-done | bytes 532512 | tf_op jit(solution)/shard_map/ppermute | solution.py:262
  64.8 1.4 %fusion = f32[2048,128]{1,0:T(8,128)} fusion(f32[2048,128]{1,0:T(8,128)S(1)} %shard_map.80, s16[2080,128]{1,0:T(8,128)(2,1)S(1)} %collective-permute-done.4, s16[2080,128]{1,0:T(8,128)(2,1)S(1)} %collective-permute-done.3, f32[32,128]{1,0:T(8,128)S(1)} %exponential_multiply_fusion, f32[32,128]{1,0:T(8,128)S(1)} %exponential_multiply_fusion.1), kind=kLoop, calls=%fused_computation.1 | loop fusion | flops 1572864 | bytes 3178496 | tf_op jit(solution)/shard_map/add | solution.py:269
  (2 shorter events, 0.0 us)
Async XLA Ops:
  0.0 22.7 %collective-permute-start = (bf16[8,8,40,128]{3,2,1,0:T(8,128)(2,1)}, bf16[8,8,40,128]{3,2,1,0:T(8,128)(2,1)S(1)}, u32[]{:S(2)}, u32[]{:S(2)}) collective-permute-start(bf16[8,8,40,128]{3,2,1,0:T(8,128)(2,1)} %bitcast.23), channel_id=1, source_target_pairs={{0,1},{1,0},{2,3},{3,2},{4,5},{5,4},{6,7},{7,6},{8,9},{9,8},{10,11... | collective-permute-start | bytes 1966088 | tf_op jit(solution)/shard_map/ppermute | solution.py:184
  3.9 1.1 %copy-start.2 = (bf16[1,8,8,40,128]{4,3,2,1,0:T(8,128)(2,1)S(1)}, bf16[1,8,8,40,128]{4,3,2,1,0:T(8,128)(2,1)}, u32[]{:S(2)}) copy-start(bf16[1,8,8,40,128]{4,3,2,1,0:T(8,128)(2,1)} %param.7) | copy-start | bytes 1966084
  27.5 11.2 %copy-start = (f32[2048,128]{1,0:T(8,128)S(1)}, f32[2048,128]{1,0:T(8,128)}, u32[]{:S(2)}) copy-start(f32[2048,128]{1,0:T(8,128)} %get-tuple-element.30.init) | copy-start | bytes 3145732
  31.4 7.3 %collective-permute-start.1 = (f32[2048,128]{1,0:T(8,128)S(1)}, f32[2048,128]{1,0:T(8,128)S(1)}, u32[]{:S(2)}, u32[]{:S(2)}) collective-permute-start(f32[2048,128]{1,0:T(8,128)S(1)} %shard_map.77), channel_id=1, source_target_pairs={{0,2},{2,0},{4,6},{6,4},{8,10},{10,8},{12,14},{14,12},{16,18},{18,... | collective-permute-start | bytes 3145736 | tf_op jit(solution)/shard_map/ppermute | solution.py:258
  31.5 22.7 %copy-start.1 = (f32[2048,128]{1,0:T(8,128)S(1)}, f32[2048,128]{1,0:T(8,128)}, u32[]{:S(2)}) copy-start(f32[2048,128]{1,0:T(8,128)} %get-tuple-element.33.init) | copy-start | bytes 3145732
  36.6 17.5 %collective-permute-start.2 = (f32[2048,128]{1,0:T(8,128)S(1)}, f32[2048,128]{1,0:T(8,128)S(1)}, u32[]{:S(2)}, u32[]{:S(2)}) collective-permute-start(f32[2048,128]{1,0:T(8,128)S(1)} %shard_map.78), channel_id=1, source_target_pairs={{0,2},{2,0},{4,6},{6,4},{8,10},{10,8},{12,14},{14,12},{16,18},{18,... | collective-permute-start | bytes 3145736 | tf_op jit(solution)/shard_map/ppermute | solution.py:260
  36.7 17.4 %collective-permute-start.3 = (s16[2080,128]{1,0:T(8,128)(2,1)S(1)}, s16[2080,128]{1,0:T(8,128)(2,1)S(1)}, u32[]{:S(2)}, u32[]{:S(2)}) collective-permute-start(s16[2080,128]{1,0:T(8,128)(2,1)S(1)} %shard_map.76), channel_id=1, source_target_pairs={{2,6},{4,0},{6,10},{8,4},{10,14},{12,8},{14,18},{16,12},{18,22},{2... | collective-permute-start | bytes 1597448 | tf_op jit(solution)/shard_map/ppermute | solution.py:256
  41.9 22.8 %collective-permute-start.4 = (s16[2080,128]{1,0:T(8,128)(2,1)S(1)}, s16[2080,128]{1,0:T(8,128)(2,1)S(1)}, u32[]{:S(2)}, u32[]{:S(2)}) collective-permute-start(s16[2080,128]{1,0:T(8,128)(2,1)S(1)} %shard_map.79), channel_id=1, source_target_pairs={{2,4},{4,2},{6,8},{8,6},{10,12},{12,10},{14,16},{16,14},{18,20},{2... | collective-permute-start | bytes 1597448 | tf_op jit(solution)/shard_map/ppermute | solution.py:262
where the time goes:
time: 65.3 us; the launch traced here: 66.1 us
  Pallas kernels  39.3 us (60%)
  waiting for transfers between devices  14.4 us (22%)
  starting transfers between devices  6.08 us (9%)
  local copies, waits for them, and re-layouts  3.21 us (5%)
  other arithmetic  2.98 us (5%)
    pallas_call x5, Pallas kernels, run(): pl.pallas_call(partial(rest_kernel, role=role, gates=gates, bins=bins, sl...  21 us
    pallas_call x1, Pallas kernels, local(): pl.pallas_call(partial(first_kernel, gates=gates, bins=bins, slots=slots,...  17 us
    ppermute x1, waiting for transfers between devices, local(): far = lax.ppermute(far, 'slab', outward(2))  8.43 us
    ppermute x1, waiting for transfers between devices, local(): near = lax.ppermute(near, 'slab', outward(1))  5.95 us
    ppermute x1, starting transfers between devices, local(): near = lax.ppermute(near, 'slab', outward(1))  3.76 us
    unnamed x8, local copies, waits for them, and re-layouts  2.47 us
    ppermute x1, starting transfers between devices, local(): far = lax.ppermute(far, 'slab', outward(2))  1.92 us
    add x1, other arithmetic, local(): image_sum = own + widen(far) + widen(near)  1.38 us
  transfers between devices with their start and end apart: 5, of which 2 were waited for; matrix products, arithmetic and copies ran while one was open for 6% of the time, Pallas kernels for 46%

commit v1 on v0

v1 whole, which is shorter than its diff:
```python
from functools import partial

import jax
import jax.numpy as jnp
from jax import lax
from jax.experimental import pallas as pl
from jax.experimental.pallas import tpu as pltpu
from jax.sharding import PartitionSpec as P

VT = 256
UNROLL = 4
CHUNKS = 4
GROUP = 64
TOP = 32767.0
STEPS = 8.0
LIMIT = 50 * 1024 * 1024
SMEM = pl.BlockSpec(memory_space=pltpu.SMEM)
VMEM = pl.BlockSpec(memory_space=pltpu.VMEM)
HBM = pl.BlockSpec(memory_space=pl.ANY)

FAR, IN2, NEAR, IN1, OWN = range(5)
REACH = (2, -2, 1, -1, 0)
SPLIT = 4
COST = pl.CostEstimate(flops=1000, bytes_accessed=1000, transcendentals=0)


def add_slots(acc, buf, sino, slot_of, row_of, voxel_of, begin, total, gates, bins):
    size = gates * bins
    dump = VT + bins

    def group(i, carry):
        first = begin + i * UNROLL
        outs = []
        ats = []
        for u in range(UNROLL):
            k = first + u
            live = k < total
            j = jnp.where(live, slot_of(k), 0)
            row = jnp.where(live, row_of(k, j), 0)
            v = jnp.where(live, voxel_of(j), dump)
            ats.append(pl.ds(pl.multiple_of(v * gates, gates), size))
            outs.append(jnp.dot(sino[row], buf[j], preferred_element_type=jnp.float32))
        for at, out in zip(ats, outs):
            acc[at] += out
        return carry

    lax.fori_loop(0, (total - begin + UNROLL - 1) // UNROLL, group, 0)


def list_of(role):
    sign = 2 * lax.rem(lax.axis_index("slab"), 2) - 1
    return REACH[0] + REACH[role] * sign


def place_of(row, local_rows):
    block, blocks = lax.axis_index("blk"), lax.axis_size("blk")
    hop = block - lax.div(row, local_rows)
    hop = jnp.where(hop < 0, hop + blocks, hop)
    return hop * local_rows + lax.rem(row, local_rows)


def sorter(shift, gates, bins):
    size = gates * bins
    src = lax.broadcasted_iota(jnp.int32, (1, size), 1)
    bin_of = lax.rem(src, bins)
    place = jnp.zeros((1, size), jnp.int32)
    for t in range(bins):
        place = jnp.where(bin_of == t, shift[t] + bins // 2, place)
    target = place * gates + lax.div(src, bins)
    dst = lax.broadcasted_iota(jnp.int32, (size, size), 0)
    return (target == dst).astype(jnp.float32).astype(jnp.bfloat16)


def reorder(mat, tile):
    return jnp.dot(mat, tile, preferred_element_type=jnp.float32).astype(jnp.bfloat16)


def join_kernel(shift, mine, others, out, *, gates, bins):
    mat = sorter(shift, gates, bins)
    local_rows = mine.shape[0]
    out[0:local_rows] = mine[...]

    def one(i, carry):
        out[local_rows + i] = reorder(mat, others[i])
        return carry

    lax.fori_loop(0, others.shape[0], one, 0, unroll=4)


def first_kernel(
    shift, counts, rows, voxels, res, tiles, *rest, gates, bins, slots
):
    *parts, sino, far_slots, far_rows, far_counts, raw, acc, buf, near_slots, raw_sem, sems = rest
    local_rows = res.shape[0]
    per = slots // CHUNKS
    lead = bins // 2 * gates
    span = VT * gates

    load = pltpu.make_async_copy(res, raw, raw_sem)
    load.start()

    def chunk_copy(r, c):
        return pltpu.make_async_copy(
            tiles.at[list_of(r), pl.ds(c * per, per)], buf.at[r, pl.ds(c * per, per)], sems.at[r, c]
        )

    for r in range(SPLIT):
        for c in range(CHUNKS):
            @pl.when(c * per < counts[list_of(r)])
            def _():
                chunk_copy(r, c).start()

    mat = sorter(shift, gates, bins)
    load.wait()
    for i in range(local_rows):
        sino[i] = reorder(mat, raw[i])

    for r in range(SPLIT):
        which = list_of(r)
        count = counts[which]

        def split(j, found):
            here, there = found
            row = place_of(rows[which, j], local_rows)
            near_slots[here] = j
            far_slots[r, there] = j
            far_rows[r, there] = row
            step = (row < local_rows).astype(jnp.int32)
            return here + step, there + 1 - step

        here, there = lax.fori_loop(0, count, split, (0, 0))
        far_counts[r] = there
        acc[...] = jnp.zeros(acc.shape, jnp.float32)
        for c in range(CHUNKS):
            @pl.when(c * per < count)
            def _():
                chunk_copy(r, c).wait()
        add_slots(
            acc, buf.at[r], sino, lambda k: near_slots[k],
            lambda k, j: lax.rem(rows[which, j], local_rows), lambda j: voxels[which, j],
            0, here, gates, bins,
        )
        parts[r][...] = acc[lead:lead + span]


def rest_kernel(
    counts, rows, voxels, far_slots, far_rows, far_counts, sino, tiles, *rest,
    role, gates, bins, slots, send, starts, local_rows
):
    starts_in, (out, acc, buf, sems) = rest[:starts], rest[starts:]
    which = list_of(role)
    count = counts[which]
    per = slots // CHUNKS
    lead = bins // 2 * gates
    span = VT * gates

    def chunk_copy(c):
        return pltpu.make_async_copy(
            tiles.at[which, pl.ds(c * per, per)], buf.at[pl.ds(c * per, per)], sems.at[c]
        )

    for c in range(CHUNKS):
        @pl.when(c * per < count)
        def _():
            chunk_copy(c).start()

    acc[0:lead] = jnp.zeros((lead, acc.shape[1]), jnp.float32)
    acc[lead + span:] = jnp.zeros((acc.shape[0] - lead - span, acc.shape[1]), jnp.float32)
    if starts == 0:
        acc[lead:lead + span] = jnp.zeros((span, acc.shape[1]), jnp.float32)
    elif starts == 1:
        acc[lead:lead + span] = starts_in[0][...]
    else:
        acc[lead:lead + span] = starts_in[0][...] + starts_in[1][...]
    for c in range(CHUNKS):
        @pl.when(c * per < count)
        def _():
            chunk_copy(c).wait()
            if role >= SPLIT:
                add_slots(
                    acc, buf, sino, lambda k: k, lambda k, j: place_of(rows[which, j], local_rows),
                    lambda j: voxels[which, j], c * per, jnp.minimum(count, (c + 1) * per), gates, bins,
                )
    if role < SPLIT:
        add_slots(
            acc, buf, sino, lambda k: far_slots[role, k], lambda k, j: far_rows[role, k],
            lambda j: voxels[which, j], 0, far_counts[role], gates, bins,
        )
    if send:
        groups = span // GROUP
        vals = acc[lead:lead + span].reshape(groups, GROUP, acc.shape[1])
        top = jnp.maximum(jnp.max(jnp.abs(vals), axis=1), 1e-30)
        code = jnp.ceil(STEPS * jnp.log2(top))
        inv = TOP * jnp.exp2(code * (-1.0 / STEPS))
        q = jnp.clip(jnp.round(vals * inv[:, None, :]), -TOP, TOP)
        out[0:span] = q.astype(jnp.int32).astype(jnp.int16).reshape(span, acc.shape[1])
        out[span:] = code.astype(jnp.int32).astype(jnp.int16)
    else:
        out[...] = acc[lead:lead + span]


def join_image(own, far, near, out):
    span, width = own.shape
    groups = span // GROUP

    def widen(sent):
        code = sent[span:].astype(jnp.int32).astype(jnp.float32)
        scale = jnp.exp2(code * (1.0 / STEPS)) * (1.0 / TOP)
        values = sent[0:span].astype(jnp.int32).astype(jnp.float32).reshape(groups, GROUP, width)
        return (values * scale[:, None, :]).reshape(span, width)

    out[...] = own[...] + widen(far) + widen(near)


def local(residual, tile_values, row_index, voxel_index, slot_count, tof_shift):
    local_rows, gates, bins, depth = residual.shape[1:]
    lists, slots, _, width = tile_values.shape[2:]
    size = gates * bins
    span = VT * gates
    tiles = tile_values[0, 0]
    rows = row_index[0, 0]
    voxels = voxel_index[0, 0]
    counts = slot_count[0, 0]
    slabs = lax.axis_size("slab")
    blocks = lax.axis_size("blk")
    res = residual[0].reshape(local_rows, size, depth)
    others = [
        lax.ppermute(res, "blk", [(i, (i + hop) % blocks) for i in range(blocks)])
        for hop in range(1, blocks)
    ]
    params = pltpu.CompilerParams(vmem_limit_bytes=LIMIT)

    acc = pltpu.VMEM((span + bins * gates + size, width), jnp.float32)
    image = jax.ShapeDtypeStruct((span, width), jnp.float32)
    table = jax.ShapeDtypeStruct((SPLIT, slots), jnp.int32)
    *parts, mine, far_slots, far_rows, far_counts = pl.pallas_call(
        partial(first_kernel, gates=gates, bins=bins, slots=slots),
        out_shape=[image] * SPLIT
        + [jax.ShapeDtypeStruct(res.shape, res.dtype)]
        + [table, table, jax.ShapeDtypeStruct((SPLIT,), jnp.int32)],
        in_specs=[SMEM] * 4 + [HBM, HBM],
        out_specs=[VMEM] * (SPLIT + 1) + [SMEM] * 3,
        scratch_shapes=[
            pltpu.VMEM(res.shape, res.dtype),
            acc,
            pltpu.VMEM((SPLIT, slots, depth, width), jnp.bfloat16),
            pltpu.SMEM((slots,), jnp.int32),
            pltpu.SemaphoreType.DMA(()),
            pltpu.SemaphoreType.DMA((SPLIT, CHUNKS)),
        ],
        compiler_params=params,
        cost_estimate=COST,
    )(tof_shift, counts, rows, voxels, res, tiles)

    sino = pl.pallas_call(
        partial(join_kernel, gates=gates, bins=bins),
        out_shape=jax.ShapeDtypeStruct((local_rows * blocks, size, depth), jnp.bfloat16),
        in_specs=[SMEM, VMEM, VMEM],
        out_specs=VMEM,
        compiler_params=params,
        cost_estimate=COST,
    )(tof_shift, mine, others[0] if len(others) == 1 else jnp.concatenate(others))

    def run(role, after, got=None):
        send = role in (FAR, NEAR)
        held = counts
        if after is not None:
            held, after = lax.optimization_barrier((counts, after))
        starts = [parts[role]] if role < SPLIT else []
        starts += [] if got is None else [got]
        out = pl.pallas_call(
            partial(
                rest_kernel, role=role, gates=gates, bins=bins, slots=slots, send=send,
                starts=len(starts), local_rows=local_rows,
            ),
            out_shape=(
                jax.ShapeDtypeStruct((span + span // GROUP, width), jnp.int16) if send else image
            ),
            in_specs=[SMEM] * 6 + [VMEM, HBM] + [VMEM] * len(starts),
            out_specs=VMEM,
            scratch_shapes=[
                acc,
                pltpu.VMEM((slots, depth, width), jnp.bfloat16),
                pltpu.SemaphoreType.DMA((CHUNKS,)),
            ],
            compiler_params=params,
            cost_estimate=COST,
        )(held, rows, voxels, far_slots, far_rows, far_counts, sino, tiles, *starts)
        return out, after

    mate = [(i, i ^ 1) for i in range(slabs)]

    def outward(distance):
        route = []
        for i in range(slabs):
            j = i + (distance if i % 2 else -distance)
            if 0 <= j < slabs:
                route.append((i, j))
        return route

    in2, _ = run(IN2, None)
    in1, in2 = run(IN1, in2)
    in2 = lax.ppermute(in2, "slab", mate)
    far, in1 = run(FAR, in1)
    in1 = lax.ppermute(in1, "slab", mate)
    near, far = run(NEAR, far, in2)
    far = lax.ppermute(far, "slab", outward(2))
    own, near = run(OWN, near, in1)
    near = lax.ppermute(near, "slab", outward(1))
    image_sum = pl.pallas_call(
        join_image,
        out_shape=image,
        in_specs=[VMEM] * 3,
        out_specs=VMEM,
        compiler_params=params,
        cost_estimate=COST,
    )(own, far, near)
    return image_sum.reshape(1, VT, gates, width)


def solution(mesh):
    placed = (
        P("slab", "blk", None, None, None),
        P("slab", "blk", None, None, None, None),
        P("slab", "blk", None, None),
        P("slab", "blk", None, None),
        P("slab", "blk", None),
        P(),
    )
    return jax.shard_map(
        local, mesh=mesh, in_specs=placed, out_specs=P("slab", "blk", None, None), check_vma=False
    )
```

time: 65.3 us -> 61.4 us (0.940)
  the two profiles are of different devices: /device:TPU:11 before, /device:TPU:9 now
where the time goes in v1:
time: 61.4 us; the launch traced here: 61.1 us
  Pallas kernels  36.8 us (60%)
  waiting for transfers between devices  13.5 us (22%)
  starting transfers between devices  7.64 us (12%)
  local copies, waits for them, and re-layouts  3.1 us (5%)
    pallas_call x5, Pallas kernels, run(): pl.pallas_call(partial(rest_kernel, role=role, gates=gates, bins=bins, sl...  21.3 us
    pallas_call x1, Pallas kernels, local(): pl.pallas_call(partial(first_kernel, gates=gates, bins=bins, slots=slots)...  12.7 us
    ppermute x1, waiting for transfers between devices, local(): near = lax.ppermute(near, 'slab', outward(1))  7.64 us
    ppermute x1, waiting for transfers between devices, local(): far = lax.ppermute(far, 'slab', outward(2))  5.87 us
    unnamed x11, local copies, waits for them, and re-layouts  3.1 us
    ppermute x1, starting transfers between devices, local(): in2 = lax.ppermute(in2, 'slab', mate)  2.49 us
    ppermute x1, starting transfers between devices, local(): near = lax.ppermute(near, 'slab', outward(1))  1.94 us
    ppermute x1, starting transfers between devices, local(): far = lax.ppermute(far, 'slab', outward(2))  1.92 us
  transfers between devices with their start and end apart: 5, of which 2 were waited for; matrix products, arithmetic and copies ran while one was open for 1% of the time, Pallas kernels for 50%

profile of v1, /device:TPU:9, one launch (start us, length us, event | category | flops | bytes accessed | tf_op | source)
XLA Modules:
  0.0 61.1 jit_solution(13558498002019345053)
XLA Ops:
  0.0 1.2 %collective-permute-start = (bf16[8,320,128]{2,1,0:T(8,128)(2,1)}, bf16[8,320,128]{2,1,0:T(8,128)(2,1)S(1)}, u32[]{:S(2)}, u32[]{:S(2)}) collective-permute-start(bf16[8,320,128]{2,1,0:T(8,128)(2,1)} %bitcast.8), channel_id=1, source_target_pairs={{0,1},{1,0},{2,3},{3,2},{4,5},{5,4},{6,7},{7,6},{8,9},{9,8},{10,11... | collective-permute-start | bytes 1966088 | tf_op jit(solution)/shard_map/ppermute | solution.py:228
  1.2 0.7 %copy_bitcast_fusion = (s32[5,64]{1,0:T(8,128)S(1)}, s32[5,64]{1,0:T(8,128)S(1)}) fusion(s32[1,1,5,64]{3,1,2,0:T(1,128)} %param.9, s32[1,1,5,64]{3,1,2,0:T(1,128)} %param.8), kind=kLoop, calls=%fused_computation | loop fusion | bytes 5120
  1.9 0.0 copy-start.2
  1.9 1.1 %copy-done.2 = bf16[1,8,8,40,128]{4,3,2,1,0:T(8,128)(2,1)S(1)} copy-done((bf16[1,8,8,40,128]{4,3,2,1,0:T(8,128)(2,1)S(1)}, bf16[1,8,8,40,128]{4,3,2,1,0:T(8,128)(2,1)}, u32[]{:S(2)}) %copy-start.2) | copy-done | bytes 655384
  3.0 0.0 copy-start.3
  3.0 0.7 %copy-done.3 = s32[1,1,5]{2,1,0:T(1,128)S(1)} copy-done((s32[1,1,5]{2,1,0:T(1,128)S(1)}, s32[1,1,5]{2,1,0:T(1,128)}, u32[]{:S(2)}) %copy-start.3) | copy-done | bytes 44
  3.7 0.0 copy-start.4
  3.7 0.7 %copy-done.4 = s32[40]{0:T(128)S(1)} copy-done((s32[40]{0:T(128)S(1)}, s32[40]{0:T(128)}, u32[]{:S(2)}) %copy-start.4) | copy-done | bytes 184
  4.3 12.7 %shard_map.64 = (f32[2048,128]{1,0:T(8,128)S(1)}, f32[2048,128]{1,0:T(8,128)S(1)}, f32[2048,128]{1,0:T(8,128)}, f32[2048,128]{1,0:T(8,128)}, bf16[8,320,128]{2,1...) custom-call(s32[40]{0:T(128)S(1)} %copy-done.4, s32[5]{0:T(128)S(1)} %bitcast.10, ...), custom_call_target="tpu_custom_call" | custom-call | flops 1000 | bytes 1000 | tf_op jit(solution)/shard_map/pallas_call | solution.py:236
  17.1 0.0 copy-start.1
  17.1 0.0 collective-permute-done.others
  17.1 1.5 %shard_map.65.sino = bf16[16,320,128]{2,1,0:T(8,128)(2,1)S(1)} custom-call(s32[40]{0:T(128)S(1)} %copy-done.4, bf16[8,320,128]{2,1,0:T(8,128)(2,1)S(1)} %get-tuple-element.24.mine, bf16[8,320,128]{2,1,0:T(8,128)(2,1)S(1)} %collective-permute-done.others), custom_call_target="tpu_custom_call" | custom-call | flops 1000 | bytes 1000 | tf_op jit(solution)/shard_map/pallas_call | solution.py:255
  18.6 3.5 %shard_map.66 = f32[2048,128]{1,0:T(8,128)S(1)} custom-call(s32[5]{0:T(128)S(1)} %bitcast.11, s32[5,64]{1,0:T(8,128)S(1)} %get-tuple-element.38.rows, s32[5,64]{1,0:T(8,128)S(1)} %get-tuple-element.37.voxels, s32[4,64]{1,0:T(4,128)S(1)} %get-tuple-element.21.far_slots, s32[4,64]{1,0:T(4,128)S(1)} %get-tuple-element.22.far_rows, ...), custom_call_target="tpu_custom_call" | custom-call | flops 1000 | bytes 1000 | tf_op jit(solution)/shard_map/pallas_call | solution.py:271
  22.1 2.5 %collective-permute-start.1 = (f32[2048,128]{1,0:T(8,128)S(1)}, f32[2048,128]{1,0:T(8,128)S(1)}, u32[]{:S(2)}, u32[]{:S(2)}) collective-permute-start(f32[2048,128]{1,0:T(8,128)S(1)} %shard_map.66), channel_id=1, source_target_pairs={{0,2},{2,0},{4,6},{6,4},{8,10},{10,8},{12,14},{14,12},{16,18},{18,... | collective-permute-start | bytes 3145736 | tf_op jit(solution)/shard_map/ppermute | solution.py:303
  24.5 0.0 copy-done.1
  24.6 0.0 copy-start
  24.6 4.1 %shard_map.67 = f32[2048,128]{1,0:T(8,128)S(1)} custom-call(s32[5]{0:T(128)S(1)} %bitcast.12, s32[5,64]{1,0:T(8,128)S(1)} %get-tuple-element.38.rows, s32[5,64]{1,0:T(8,128)S(1)} %get-tuple-element.37.voxels, s32[4,64]{1,0:T(4,128)S(1)} %get-tuple-element.21.far_slots, s32[4,64]{1,0:T(4,128)S(1)} %get-tuple-element.22.far_rows, ...), custom_call_target="tpu_custom_call" | custom-call | flops 1000 | bytes 1000 | tf_op jit(solution)/shard_map/pallas_call | solution.py:271
  28.7 0.1 collective-permute-start.2
  28.8 3.9 %shard_map.68 = s16[2080,128]{1,0:T(8,128)(2,1)S(1)} custom-call(s32[5]{0:T(128)S(1)} %bitcast.13, s32[5,64]{1,0:T(8,128)S(1)} %get-tuple-element.38.rows, s32[5,64]{1,0:T(8,128)S(1)} %get-tuple-element.37.voxels, s32[4,64]{1,0:T(4,128)S(1)} %get-tuple-element.21.far_slots, s32[4,64]{1,0:T(4,128)S(1)} %get-tuple-element.22.far_rows, ...), custom_call_target="tpu_custom_call" | custom-call | flops 1000 | bytes 1000 | tf_op jit(solution)/shard_map/pallas_call | solution.py:271
  32.7 1.9 %collective-permute-start.3 = (s16[2080,128]{1,0:T(8,128)(2,1)S(1)}, s16[2080,128]{1,0:T(8,128)(2,1)S(1)}, u32[]{:S(2)}, u32[]{:S(2)}) collective-permute-start(s16[2080,128]{1,0:T(8,128)(2,1)S(1)} %shard_map.68), channel_id=1, source_target_pairs={{2,6},{4,0},{6,10},{8,4},{10,14},{12,8},{14,18},{16,12},{18,22},{2... | collective-permute-start | bytes 1597448 | tf_op jit(solution)/shard_map/ppermute | solution.py:307
  34.6 0.0 collective-permute-done.1.rest_1_
  34.6 0.0 copy-done
  34.6 4.6 %shard_map.69 = s16[2080,128]{1,0:T(8,128)(2,1)S(1)} custom-call(s32[5]{0:T(128)S(1)} %bitcast.14, s32[5,64]{1,0:T(8,128)S(1)} %get-tuple-element.38.rows, s32[5,64]{1,0:T(8,128)S(1)} %get-tuple-element.37.voxels, s32[4,64]{1,0:T(4,128)S(1)} %get-tuple-element.21.far_slots, s32[4,64]{1,0:T(4,128)S(1)} %get-tuple-element.22.far_rows, ...), custom_call_target="tpu_custom_call" | custom-call | flops 1000 | bytes 1000 | tf_op jit(solution)/shard_map/pallas_call | solution.py:271
  39.2 1.9 %collective-permute-start.4 = (s16[2080,128]{1,0:T(8,128)(2,1)S(1)}, s16[2080,128]{1,0:T(8,128)(2,1)S(1)}, u32[]{:S(2)}, u32[]{:S(2)}) collective-permute-start(s16[2080,128]{1,0:T(8,128)(2,1)S(1)} %shard_map.69), channel_id=1, source_target_pairs={{2,4},{4,2},{6,8},{8,6},{10,12},{12,10},{14,16},{16,14},{18,20},{2... | collective-permute-start | bytes 1597448 | tf_op jit(solution)/shard_map/ppermute | solution.py:309
  41.2 0.0 collective-permute-done.2.rest_0_
  41.2 5.1 %shard_map.70.own = f32[2048,128]{1,0:T(8,128)S(1)} custom-call(s32[5]{0:T(128)S(1)} %bitcast.15, s32[5,64]{1,0:T(8,128)S(1)} %get-tuple-element.38.rows, s32[5,64]{1,0:T(8,128)S(1)} %get-tuple-element.37.voxels, s32[4,64]{1,0:T(4,128)S(1)} %get-tuple-element.21.far_slots, s32[4,64]{1,0:T(4,128)S(1)} %get-tuple-element.22.far_rows, ...), custom_call_target="tpu_custom_call" | custom-call | flops 1000 | bytes 1000 | tf_op jit(solution)/shard_map/pallas_call | solution.py:271
  46.4 5.9 %collective-permute-done.3.far = s16[2080,128]{1,0:T(8,128)(2,1)S(1)} collective-permute-done((s16[2080,128]{1,0:T(8,128)(2,1)S(1)}, s16[2080,128]{1,0:T(8,128)(2,1)S(1)}, u32[]{:S(2)}, u32[]{:S(2)}) %collective-permute-start.3) | collective-permute-done | bytes 532512 | tf_op jit(solution)/shard_map/ppermute | solution.py:307
  52.2 7.6 %collective-permute-done.4.near = s16[2080,128]{1,0:T(8,128)(2,1)S(1)} collective-permute-done((s16[2080,128]{1,0:T(8,128)(2,1)S(1)}, s16[2080,128]{1,0:T(8,128)(2,1)S(1)}, u32[]{:S(2)}, u32[]{:S(2)}) %collective-permute-start.4) | collective-permute-done | bytes 532512 | tf_op jit(solution)/shard_map/ppermute | solution.py:309
  59.9 1.3 %shard_map.71 = f32[2048,128]{1,0:T(8,128)} custom-call(f32[2048,128]{1,0:T(8,128)S(1)} %shard_map.70.own, s16[2080,128]{1,0:T(8,128)(2,1)S(1)} %collective-permute-done.3.far, s16[2080,128]{1,0:T(8,128)(2,1)S(1)} %collective-permute-done.4.near), custom_call_target="tpu_custom_call" | custom-call | flops 1000 | bytes 1000 | tf_op jit(solution)/shard_map/pallas_call | solution.py:310
Async XLA Ops:
  0.0 17.1 %collective-permute-start = (bf16[8,320,128]{2,1,0:T(8,128)(2,1)}, bf16[8,320,128]{2,1,0:T(8,128)(2,1)S(1)}, u32[]{:S(2)}, u32[]{:S(2)}) collective-permute-start(bf16[8,320,128]{2,1,0:T(8,128)(2,1)} %bitcast.8), channel_id=1, source_target_pairs={{0,1},{1,0},{2,3},{3,2},{4,5},{5,4},{6,7},{7,6},{8,9},{9,8},{10,11... | collective-permute-start | bytes 1966088 | tf_op jit(solution)/shard_map/ppermute | solution.py:228
  1.9 1.1 %copy-start.2 = (bf16[1,8,8,40,128]{4,3,2,1,0:T(8,128)(2,1)S(1)}, bf16[1,8,8,40,128]{4,3,2,1,0:T(8,128)(2,1)}, u32[]{:S(2)}) copy-start(bf16[1,8,8,40,128]{4,3,2,1,0:T(8,128)(2,1)} %param.6) | copy-start | bytes 1966084
  3.0 0.7 %copy-start.3 = (s32[1,1,5]{2,1,0:T(1,128)S(1)}, s32[1,1,5]{2,1,0:T(1,128)}, u32[]{:S(2)}) copy-start(s32[1,1,5]{2,1,0:T(1,128)} %param.10) | copy-start | bytes 64
  3.7 0.7 %copy-start.4 = (s32[40]{0:T(128)S(1)}, s32[40]{0:T(128)}, u32[]{:S(2)}) copy-start(s32[40]{0:T(128)} %shift.3) | copy-start | bytes 484
  17.1 7.5 %copy-start.1 = (f32[2048,128]{1,0:T(8,128)S(1)}, f32[2048,128]{1,0:T(8,128)}, u32[]{:S(2)}) copy-start(f32[2048,128]{1,0:T(8,128)} %get-tuple-element.27.rest_0_) | copy-start | bytes 3145732
  22.1 12.6 %collective-permute-start.1 = (f32[2048,128]{1,0:T(8,128)S(1)}, f32[2048,128]{1,0:T(8,128)S(1)}, u32[]{:S(2)}, u32[]{:S(2)}) collective-permute-start(f32[2048,128]{1,0:T(8,128)S(1)} %shard_map.66), channel_id=1, source_target_pairs={{0,2},{2,0},{4,6},{6,4},{8,10},{10,8},{12,14},{14,12},{16,18},{18,... | collective-permute-start | bytes 3145736 | tf_op jit(solution)/shard_map/ppermute | solution.py:303
  24.6 10.1 %copy-start = (f32[2048,128]{1,0:T(8,128)S(1)}, f32[2048,128]{1,0:T(8,128)}, u32[]{:S(2)}) copy-start(f32[2048,128]{1,0:T(8,128)} %get-tuple-element.31.rest_0_) | copy-start | bytes 3145732
  28.7 12.5 %collective-permute-start.2 = (f32[2048,128]{1,0:T(8,128)S(1)}, f32[2048,128]{1,0:T(8,128)S(1)}, u32[]{:S(2)}, u32[]{:S(2)}) collective-permute-start(f32[2048,128]{1,0:T(8,128)S(1)} %shard_map.67), channel_id=1, source_target_pairs={{0,2},{2,0},{4,6},{6,4},{8,10},{10,8},{12,14},{14,12},{16,18},{18,... | collective-permute-start | bytes 3145736 | tf_op jit(solution)/shard_map/ppermute | solution.py:305
  32.7 19.5 %collective-permute-start.3 = (s16[2080,128]{1,0:T(8,128)(2,1)S(1)}, s16[2080,128]{1,0:T(8,128)(2,1)S(1)}, u32[]{:S(2)}, u32[]{:S(2)}) collective-permute-start(s16[2080,128]{1,0:T(8,128)(2,1)S(1)} %shard_map.68), channel_id=1, source_target_pairs={{2,6},{4,0},{6,10},{8,4},{10,14},{12,8},{14,18},{16,12},{18,22},{2... | collective-permute-start | bytes 1597448 | tf_op jit(solution)/shard_map/ppermute | solution.py:307
  39.2 20.6 %collective-permute-start.4 = (s16[2080,128]{1,0:T(8,128)(2,1)S(1)}, s16[2080,128]{1,0:T(8,128)(2,1)S(1)}, u32[]{:S(2)}, u32[]{:S(2)}) collective-permute-start(s16[2080,128]{1,0:T(8,128)(2,1)S(1)} %shard_map.69), channel_id=1, source_target_pairs={{2,4},{4,2},{6,8},{8,6},{10,12},{12,10},{14,16},{16,14},{18,20},{2... | collective-permute-start | bytes 1597448 | tf_op jit(solution)/shard_map/ppermute | solution.py:309

commit v2 on v1

--- a/solution.py
+++ b/solution.py
@@ -20,7 +20,8 @@
 
 FAR, IN2, NEAR, IN1, OWN = range(5)
 REACH = (2, -2, 1, -1, 0)
-SPLIT = 4
+PIECES = 2
+SPLIT = 3
 COST = pl.CostEstimate(flops=1000, bytes_accessed=1000, transcendentals=0)
 
 
@@ -145,9 +146,9 @@
 
 def rest_kernel(
     counts, rows, voxels, far_slots, far_rows, far_counts, sino, tiles, *rest,
-    role, gates, bins, slots, send, starts, local_rows
+    role, gates, bins, slots, send, starts, gots, local_rows
 ):
-    starts_in, (out, acc, buf, sems) = rest[:starts], rest[starts:]
+    first, got, (*out, acc, buf, sems) = rest[:starts], rest[starts:starts + gots], rest[starts + gots:]
     which = list_of(role)
     count = counts[which]
     per = slots // CHUNKS
@@ -166,12 +167,13 @@
 
     acc[0:lead] = jnp.zeros((lead, acc.shape[1]), jnp.float32)
     acc[lead + span:] = jnp.zeros((acc.shape[0] - lead - span, acc.shape[1]), jnp.float32)
-    if starts == 0:
+    if starts:
+        acc[lead:lead + span] = first[0][...]
+    else:
         acc[lead:lead + span] = jnp.zeros((span, acc.shape[1]), jnp.float32)
-    elif starts == 1:
-        acc[lead:lead + span] = starts_in[0][...]
-    else:
-        acc[lead:lead + span] = starts_in[0][...] + starts_in[1][...]
+    for i, piece in enumerate(got):
+        size = span // gots
+        acc[lead + i * size:lead + (i + 1) * size] += widen(piece)
     for c in range(CHUNKS):
         @pl.when(c * per < count)
         def _():
@@ -186,30 +188,40 @@
             acc, buf, sino, lambda k: far_slots[role, k], lambda k, j: far_rows[role, k],
             lambda j: voxels[which, j], 0, far_counts[role], gates, bins,
         )
-    if send:
-        groups = span // GROUP
-        vals = acc[lead:lead + span].reshape(groups, GROUP, acc.shape[1])
-        top = jnp.maximum(jnp.max(jnp.abs(vals), axis=1), 1e-30)
-        code = jnp.ceil(STEPS * jnp.log2(top))
-        inv = TOP * jnp.exp2(code * (-1.0 / STEPS))
-        q = jnp.clip(jnp.round(vals * inv[:, None, :]), -TOP, TOP)
-        out[0:span] = q.astype(jnp.int32).astype(jnp.int16).reshape(span, acc.shape[1])
-        out[span:] = code.astype(jnp.int32).astype(jnp.int16)
+    if not send:
+        out[0][...] = acc[lead:lead + span]
     else:
-        out[...] = acc[lead:lead + span]
-
-
-def join_image(own, far, near, out):
-    span, width = own.shape
-    groups = span // GROUP
-
-    def widen(sent):
-        code = sent[span:].astype(jnp.int32).astype(jnp.float32)
-        scale = jnp.exp2(code * (1.0 / STEPS)) * (1.0 / TOP)
-        values = sent[0:span].astype(jnp.int32).astype(jnp.float32).reshape(groups, GROUP, width)
-        return (values * scale[:, None, :]).reshape(span, width)
-
+        for i, piece in enumerate(out):
+            size = span // len(out)
+            encode(acc[lead + i * size:lead + (i + 1) * size], piece)
+
+
+def encode(image, out):
+    span, width = image.shape
+    values = image.reshape(span // GROUP, GROUP, width)
+    top = jnp.maximum(jnp.max(jnp.abs(values), axis=1), 1e-30)
+    code = jnp.ceil(STEPS * jnp.log2(top))
+    inv = TOP * jnp.exp2(code * (-1.0 / STEPS))
+    q = jnp.clip(jnp.round(values * inv[:, None, :]), -TOP, TOP)
+    out[0:span] = q.astype(jnp.int32).astype(jnp.int16).reshape(span, width)
+    out[span:] = code.astype(jnp.int32).astype(jnp.int16)
+
+
+def widen(sent):
+    span, width = sent.shape[0] * GROUP // (GROUP + 1), sent.shape[1]
+    code = sent[span:].astype(jnp.int32).astype(jnp.float32)
+    scale = jnp.exp2(code * (1.0 / STEPS)) * (1.0 / TOP)
+    values = sent[0:span].astype(jnp.int32).astype(jnp.float32)
+    values = values.reshape(span // GROUP, GROUP, width) * scale[:, None, :]
+    return values.reshape(span, width)
+
+
+def join_image(own, far, near, *rest):
+    *pair, out = rest
+    size = own.shape[0] // len(pair)
     out[...] = own[...] + widen(far) + widen(near)
+    for i, piece in enumerate(pair):
+        out[i * size:(i + 1) * size] += widen(piece)
 
 
 def local(residual, tile_values, row_index, voxel_index, slot_count, tof_shift):
@@ -261,23 +273,22 @@
         cost_estimate=COST,
     )(tof_shift, mine, others[0] if len(others) == 1 else jnp.concatenate(others))
 
-    def run(role, after, got=None):
-        send = role in (FAR, NEAR)
+    def run(role, after, got=()):
         held = counts
         if after is not None:
             held, after = lax.optimization_barrier((counts, after))
         starts = [parts[role]] if role < SPLIT else []
-        starts += [] if got is None else [got]
+        pieces = {OWN: 0, IN1: PIECES, IN2: PIECES}.get(role, 1)
+        rows_out = span // max(pieces, 1)
+        shape = jax.ShapeDtypeStruct((rows_out + rows_out // GROUP, width), jnp.int16)
         out = pl.pallas_call(
             partial(
-                rest_kernel, role=role, gates=gates, bins=bins, slots=slots, send=send,
-                starts=len(starts), local_rows=local_rows,
+                rest_kernel, role=role, gates=gates, bins=bins, slots=slots, send=pieces > 0,
+                starts=len(starts), gots=len(got), local_rows=local_rows,
             ),
-            out_shape=(
-                jax.ShapeDtypeStruct((span + span // GROUP, width), jnp.int16) if send else image
-            ),
-            in_specs=[SMEM] * 6 + [VMEM, HBM] + [VMEM] * len(starts),
-            out_specs=VMEM,
+            out_shape=[shape] * pieces if pieces else [image],
+            in_specs=[SMEM] * 6 + [VMEM, HBM] + [VMEM] * (len(starts) + len(got)),
+            out_specs=[VMEM] * max(pieces, 1),
             scratch_shapes=[
                 acc,
                 pltpu.VMEM((slots, depth, width), jnp.bfloat16),
@@ -285,8 +296,11 @@
             ],
             compiler_params=params,
             cost_estimate=COST,
-        )(held, rows, voxels, far_slots, far_rows, far_counts, sino, tiles, *starts)
+        )(held, rows, voxels, far_slots, far_rows, far_counts, sino, tiles, *starts, *got)
         return out, after
+
+    def pass_on(sent, route):
+        return [lax.ppermute(piece, "slab", route) for piece in sent]
 
     mate = [(i, i ^ 1) for i in range(slabs)]
 
@@ -299,22 +313,21 @@
         return route
 
     in2, _ = run(IN2, None)
-    in1, in2 = run(IN1, in2)
-    in2 = lax.ppermute(in2, "slab", mate)
-    far, in1 = run(FAR, in1)
-    in1 = lax.ppermute(in1, "slab", mate)
-    near, far = run(NEAR, far, in2)
-    far = lax.ppermute(far, "slab", outward(2))
-    own, near = run(OWN, near, in1)
-    near = lax.ppermute(near, "slab", outward(1))
+    far, in2 = run(FAR, in2)
+    near, far = run(NEAR, far, pass_on(in2, mate))
+    far = pass_on(far, outward(2))
+    in1, near = run(IN1, near)
+    near = pass_on(near, outward(1))
+    own, in1 = run(OWN, in1)
+    in1 = pass_on(in1, mate)
     image_sum = pl.pallas_call(
         join_image,
         out_shape=image,
-        in_specs=[VMEM] * 3,
+        in_specs=[VMEM] * (3 + PIECES),
         out_specs=VMEM,
         compiler_params=params,
         cost_estimate=COST,
-    )(own, far, near)
+    )(*own, *far, *near, *in1)
     return image_sum.reshape(1, VT, gates, width)
 
 

time: 61.4 us -> 57.4 us (0.935)
  Pallas kernels: 36.8 us -> 31.8 us
  starting transfers between devices: 7.64 us -> 10.9 us
  waiting for transfers between devices: 13.5 us -> 11.2 us
    ppermute x4 -> x6, waiting for transfers between devices: 13.5 us -> 6.89 us  [pass_on(): return [lax.ppermute(piece, 'slab', route) for piece in sent]]
    pallas_call x1, Pallas kernels: 12.7 us -> 7.19 us  [local(): pl.pallas_call(partial(first_kernel, gates=gates, bins=bins, slots=slots)...]
    ppermute x1, waiting for transfers between devices: 0.01 us -> 4.31 us  [local(): lax.ppermute(res, 'blk', [(i, (i + hop) % blocks) for i in range(blocks)])]
    ppermute x4 -> x6, starting transfers between devices: 6.43 us -> 9.73 us  [pass_on(): return [lax.ppermute(piece, 'slab', route) for piece in sent]]
    unnamed x11 -> x9, local copies, waits for them, and re-layouts: 3.1 us -> 3.1 us
  transfers between devices with their start and end apart: 5 -> 7, of which waited for: 2 -> 2; matrix products, arithmetic and copies ran while one was open for 1% -> 1% of each run, Pallas kernels for 50% -> 45%
where the time goes in v2:
time: 57.4 us; the launch traced here: 57.2 us
  Pallas kernels  31.8 us (55%)
  waiting for transfers between devices  11.2 us (20%)
  starting transfers between devices  10.9 us (19%)
  local copies, waits for them, and re-layouts  3.1 us (5%)
    pallas_call x5, Pallas kernels, run(): pl.pallas_call(partial(rest_kernel, role=role, gates=gates, bins=bins, sl...  21.2 us
    ppermute x6, starting transfers between devices, pass_on(): return [lax.ppermute(piece, 'slab', route) for piece in sent]  9.73 us
    pallas_call x1, Pallas kernels, local(): pl.pallas_call(partial(first_kernel, gates=gates, bins=bins, slots=slots)...  7.19 us
    ppermute x6, waiting for transfers between devices, pass_on(): return [lax.ppermute(piece, 'slab', route) for piece in sent]  6.89 us
    ppermute x1, waiting for transfers between devices, local(): lax.ppermute(res, 'blk', [(i, (i + hop) % blocks) for i in range(blocks)])  4.31 us
    unnamed x9, local copies, waits for them, and re-layouts  3.1 us
    pallas_call x1, Pallas kernels, local(): pl.pallas_call(join_image, out_shape=image, in_specs=[VMEM] * (3 + PIECES...  1.88 us
    pallas_call x1, Pallas kernels, local(): pl.pallas_call(partial(join_kernel, gates=gates, bins=bins), out_shape=ja...  1.47 us
  transfers between devices with their start and end apart: 7, of which 2 were waited for; matrix products, arithmetic and copies ran while one was open for 1% of the time, Pallas kernels for 45%

profile of v2, /device:TPU:9, one launch (start us, length us, event | category | flops | bytes accessed | tf_op | source)
XLA Modules:
  0.0 57.2 jit_solution(9958297987204817299)
XLA Ops:
  0.0 1.2 %collective-permute-start = (bf16[8,320,128]{2,1,0:T(8,128)(2,1)}, bf16[8,320,128]{2,1,0:T(8,128)(2,1)S(1)}, u32[]{:S(2)}, u32[]{:S(2)}) collective-permute-start(bf16[8,320,128]{2,1,0:T(8,128)(2,1)} %bitcast.8), channel_id=1, source_target_pairs={{0,1},{1,0},{2,3},{3,2},{4,5},{5,4},{6,7},{7,6},{8,9},{9,8},{10,11... | collective-permute-start | bytes 1966088 | tf_op jit(solution)/shard_map/ppermute | solution.py:240
  1.2 0.7 %copy_bitcast_fusion = (s32[5,64]{1,0:T(8,128)S(1)}, s32[5,64]{1,0:T(8,128)S(1)}) fusion(s32[1,1,5,64]{3,1,2,0:T(1,128)} %param.9, s32[1,1,5,64]{3,1,2,0:T(1,128)} %param.8), kind=kLoop, calls=%fused_computation | loop fusion | bytes 5120
  1.9 0.0 copy-start.1
  1.9 1.1 %copy-done.1 = bf16[1,8,8,40,128]{4,3,2,1,0:T(8,128)(2,1)S(1)} copy-done((bf16[1,8,8,40,128]{4,3,2,1,0:T(8,128)(2,1)S(1)}, bf16[1,8,8,40,128]{4,3,2,1,0:T(8,128)(2,1)}, u32[]{:S(2)}) %copy-start.1) | copy-done | bytes 655384
  3.0 0.0 copy-start.2
  3.0 0.7 %copy-done.2 = s32[1,1,5]{2,1,0:T(1,128)S(1)} copy-done((s32[1,1,5]{2,1,0:T(1,128)S(1)}, s32[1,1,5]{2,1,0:T(1,128)}, u32[]{:S(2)}) %copy-start.2) | copy-done | bytes 44
  3.7 0.0 copy-start.3
  3.7 0.7 %copy-done.3 = s32[40]{0:T(128)S(1)} copy-done((s32[40]{0:T(128)S(1)}, s32[40]{0:T(128)}, u32[]{:S(2)}) %copy-start.3) | copy-done | bytes 184
  4.3 7.2 %shard_map.64 = (f32[2048,128]{1,0:T(8,128)S(1)}, f32[2048,128]{1,0:T(8,128)S(1)}, f32[2048,128]{1,0:T(8,128)}, bf16[8,320,128]{2,1,0:T(8,128)(2,1)S(1)}, s32[3,...) custom-call(s32[40]{0:T(128)S(1)} %copy-done.3, s32[5]{0:T(128)S(1)} %bitcast.10, ...), custom_call_target="tpu_custom_call" | custom-call | flops 1000 | bytes 1000 | tf_op jit(solution)/shard_map/pallas_call | solution.py:248
  11.5 4.3 %collective-permute-done.others = bf16[8,320,128]{2,1,0:T(8,128)(2,1)S(1)} collective-permute-done((bf16[8,320,128]{2,1,0:T(8,128)(2,1)}, bf16[8,320,128]{2,1,0:T(8,128)(2,1)S(1)}, u32[]{:S(2)}, u32[]{:S(2)}) %collective-permute-start) | collective-permute-done | bytes 655392 | tf_op jit(solution)/shard_map/ppermute | solution.py:240
  15.8 1.5 %shard_map.65.sino = bf16[16,320,128]{2,1,0:T(8,128)(2,1)S(1)} custom-call(s32[40]{0:T(128)S(1)} %copy-done.3, bf16[8,320,128]{2,1,0:T(8,128)(2,1)S(1)} %get-tuple-element.29.mine, bf16[8,320,128]{2,1,0:T(8,128)(2,1)S(1)} %collective-permute-done.others), custom_call_target="tpu_custom_call" | custom-call | flops 1000 | bytes 1000 | tf_op jit(solution)/shard_map/pallas_call | solution.py:267
  17.3 0.0 copy-start
  17.3 2.8 %shard_map.66 = (s16[1040,128]{1,0:T(8,128)(2,1)S(1)}, s16[1040,128]{1,0:T(8,128)(2,1)S(1)}) custom-call(s32[5]{0:T(128)S(1)} %bitcast.11, s32[5,64]{1,0:T(8,128)S(1)} %get-tuple-element.48.rows, s32[5,64]{1,0:T(8,128)S(1)} %get-tuple-element.47.voxels, s32[3,64]{1,0:T(4,128)S(1)} %get-tuple-element.26.far_slots, s32[3,64]{1,0:T(4,128)S(1)} %get-tuple-element.27.far_rows, ...), custom_call_target="tpu_custom_call" | custom-call | flops 1000 | bytes 1000 | tf_op jit(solution)/shard_map/pallas_call | solution.py:284
  20.2 2.9 %collective-permute-start.1 = (s16[1040,128]{1,0:T(8,128)(2,1)S(1)}, s16[1040,128]{1,0:T(8,128)(2,1)S(1)}, u32[]{:S(2)}, u32[]{:S(2)}) collective-permute-start(s16[1040,128]{1,0:T(8,128)(2,1)S(1)} %get-tuple-element.37), channel_id=1, source_target_pairs={{0,2},{2,0},{4,6},{6,4},{8,10},{10,8},{12,14},{14,12},{16,18},{18,... | collective-permute-start | bytes 798728 | tf_op jit(solution)/shard_map/ppermute | solution.py:303
  23.1 0.1 collective-permute-start.2
  23.2 4.1 %shard_map.67 = s16[2080,128]{1,0:T(8,128)(2,1)S(1)} custom-call(s32[5]{0:T(128)S(1)} %bitcast.12, s32[5,64]{1,0:T(8,128)S(1)} %get-tuple-element.48.rows, s32[5,64]{1,0:T(8,128)S(1)} %get-tuple-element.47.voxels, s32[3,64]{1,0:T(4,128)S(1)} %get-tuple-element.26.far_slots, s32[3,64]{1,0:T(4,128)S(1)} %get-tuple-element.27.far_rows, ...), custom_call_target="tpu_custom_call" | custom-call | flops 1000 | bytes 1000 | tf_op jit(solution)/shard_map/pallas_call | solution.py:284
  27.2 2.0 %collective-permute-start.3 = (s16[2080,128]{1,0:T(8,128)(2,1)S(1)}, s16[2080,128]{1,0:T(8,128)(2,1)S(1)}, u32[]{:S(2)}, u32[]{:S(2)}) collective-permute-start(s16[2080,128]{1,0:T(8,128)(2,1)S(1)} %shard_map.67), channel_id=1, source_target_pairs={{2,6},{4,0},{6,10},{8,4},{10,14},{12,8},{14,18},{16,12},{18,22},{2... | collective-permute-start | bytes 1597448 | tf_op jit(solution)/shard_map/ppermute | solution.py:303
  29.2 0.0 collective-permute-done.1.rest_1_
  29.2 0.0 collective-permute-done.2.rest_2_
  29.2 0.0 copy-done
  29.3 3.0 %shard_map.68 = s16[2080,128]{1,0:T(8,128)(2,1)S(1)} custom-call(s32[5]{0:T(128)S(1)} %bitcast.13, s32[5,64]{1,0:T(8,128)S(1)} %get-tuple-element.48.rows, s32[5,64]{1,0:T(8,128)S(1)} %get-tuple-element.47.voxels, s32[3,64]{1,0:T(4,128)S(1)} %get-tuple-element.26.far_slots, s32[3,64]{1,0:T(4,128)S(1)} %get-tuple-element.27.far_rows, ...), custom_call_target="tpu_custom_call" | custom-call | flops 1000 | bytes 1000 | tf_op jit(solution)/shard_map/pallas_call | solution.py:284
  32.3 4.2 %collective-permute-start.4 = (s16[2080,128]{1,0:T(8,128)(2,1)S(1)}, s16[2080,128]{1,0:T(8,128)(2,1)S(1)}, u32[]{:S(2)}, u32[]{:S(2)}) collective-permute-start(s16[2080,128]{1,0:T(8,128)(2,1)S(1)} %shard_map.68), channel_id=1, source_target_pairs={{2,4},{4,2},{6,8},{8,6},{10,12},{12,10},{14,16},{16,14},{18,20},{2... | collective-permute-start | bytes 1597448 | tf_op jit(solution)/shard_map/ppermute | solution.py:303
  36.4 5.9 %shard_map.69 = (s16[1040,128]{1,0:T(8,128)(2,1)S(1)}, s16[1040,128]{1,0:T(8,128)(2,1)S(1)}) custom-call(s32[5]{0:T(128)S(1)} %bitcast.14, s32[5,64]{1,0:T(8,128)S(1)} %get-tuple-element.48.rows, s32[5,64]{1,0:T(8,128)S(1)} %get-tuple-element.47.voxels, s32[3,64]{1,0:T(4,128)S(1)} %get-tuple-element.26.far_slots, s32[3,64]{1,0:T(4,128)S(1)} %get-tuple-element.27.far_rows, ...), custom_call_target="tpu_custom_call" | custom-call | flops 1000 | bytes 1000 | tf_op jit(solution)/shard_map/pallas_call | solution.py:284
  42.3 0.1 collective-permute-start.5
  42.4 0.5 collective-permute-start.6
  42.9 5.5 %shard_map.70.own = f32[2048,128]{1,0:T(8,128)S(1)} custom-call(s32[5]{0:T(128)S(1)} %bitcast.15, s32[5,64]{1,0:T(8,128)S(1)} %get-tuple-element.48.rows, s32[5,64]{1,0:T(8,128)S(1)} %get-tuple-element.47.voxels, s32[3,64]{1,0:T(4,128)S(1)} %get-tuple-element.26.far_slots, s32[3,64]{1,0:T(4,128)S(1)} %get-tuple-element.27.far_rows, ...), custom_call_target="tpu_custom_call" | custom-call | flops 1000 | bytes 1000 | tf_op jit(solution)/shard_map/pallas_call | solution.py:284
  48.4 0.0 collective-permute-done.5.rest_0_
  48.4 0.0 collective-permute-done.6.rest_1_
  48.4 0.0 collective-permute-done.3.far
  48.4 6.9 %collective-permute-done.4.near = s16[2080,128]{1,0:T(8,128)(2,1)S(1)} collective-permute-done((s16[2080,128]{1,0:T(8,128)(2,1)S(1)}, s16[2080,128]{1,0:T(8,128)(2,1)S(1)}, u32[]{:S(2)}, u32[]{:S(2)}) %collective-permute-start.4) | collective-permute-done | bytes 532512 | tf_op jit(solution)/shard_map/ppermute | solution.py:303
  55.3 1.9 %shard_map.71 = f32[2048,128]{1,0:T(8,128)} custom-call(f32[2048,128]{1,0:T(8,128)S(1)} %shard_map.70.own, s16[2080,128]{1,0:T(8,128)(2,1)S(1)} %collective-permute-done.3.far, s16[2080,128]{1,0:T(8,128)(2,1)S(1)} %collective-permute-done.4.near, s16[1040,128]{1,0:T(8,128)(2,1)S(1)} %collective-permute-done.5.rest_0_, ...), custom_call_target="tpu_custom_call" | custom-call | flops 1000 | bytes 1000 | tf_op jit(solution)/shard_map/pallas_call | solution.py:323
Async XLA Ops:
  0.0 15.8 %collective-permute-start = (bf16[8,320,128]{2,1,0:T(8,128)(2,1)}, bf16[8,320,128]{2,1,0:T(8,128)(2,1)S(1)}, u32[]{:S(2)}, u32[]{:S(2)}) collective-permute-start(bf16[8,320,128]{2,1,0:T(8,128)(2,1)} %bitcast.8), channel_id=1, source_target_pairs={{0,1},{1,0},{2,3},{3,2},{4,5},{5,4},{6,7},{7,6},{8,9},{9,8},{10,11... | collective-permute-start | bytes 1966088 | tf_op jit(solution)/shard_map/ppermute | solution.py:240
  1.9 1.1 %copy-start.1 = (bf16[1,8,8,40,128]{4,3,2,1,0:T(8,128)(2,1)S(1)}, bf16[1,8,8,40,128]{4,3,2,1,0:T(8,128)(2,1)}, u32[]{:S(2)}) copy-start(bf16[1,8,8,40,128]{4,3,2,1,0:T(8,128)(2,1)} %param.6) | copy-start | bytes 1966084
  3.0 0.7 %copy-start.2 = (s32[1,1,5]{2,1,0:T(1,128)S(1)}, s32[1,1,5]{2,1,0:T(1,128)}, u32[]{:S(2)}) copy-start(s32[1,1,5]{2,1,0:T(1,128)} %param.10) | copy-start | bytes 64
  3.7 0.7 %copy-start.3 = (s32[40]{0:T(128)S(1)}, s32[40]{0:T(128)}, u32[]{:S(2)}) copy-start(s32[40]{0:T(128)} %shift.3) | copy-start | bytes 484
  17.3 12.0 %copy-start = (f32[2048,128]{1,0:T(8,128)S(1)}, f32[2048,128]{1,0:T(8,128)}, u32[]{:S(2)}) copy-start(f32[2048,128]{1,0:T(8,128)} %get-tuple-element.36.rest_0_) | copy-start | bytes 3145732
  20.2 9.1 %collective-permute-start.1 = (s16[1040,128]{1,0:T(8,128)(2,1)S(1)}, s16[1040,128]{1,0:T(8,128)(2,1)S(1)}, u32[]{:S(2)}, u32[]{:S(2)}) collective-permute-start(s16[1040,128]{1,0:T(8,128)(2,1)S(1)} %get-tuple-element.37), channel_id=1, source_target_pairs={{0,2},{2,0},{4,6},{6,4},{8,10},{10,8},{12,14},{14,12},{16,18},{18,... | collective-permute-start | bytes 798728 | tf_op jit(solution)/shard_map/ppermute | solution.py:303
  23.1 6.1 %collective-permute-start.2 = (s16[1040,128]{1,0:T(8,128)(2,1)S(1)}, s16[1040,128]{1,0:T(8,128)(2,1)S(1)}, u32[]{:S(2)}, u32[]{:S(2)}) collective-permute-start(s16[1040,128]{1,0:T(8,128)(2,1)S(1)} %get-tuple-element.38), channel_id=1, source_target_pairs={{0,2},{2,0},{4,6},{6,4},{8,10},{10,8},{12,14},{14,12},{16,18},{18,... | collective-permute-start | bytes 798728 | tf_op jit(solution)/shard_map/ppermute | solution.py:303
  27.2 21.1 %collective-permute-start.3 = (s16[2080,128]{1,0:T(8,128)(2,1)S(1)}, s16[2080,128]{1,0:T(8,128)(2,1)S(1)}, u32[]{:S(2)}, u32[]{:S(2)}) collective-permute-start(s16[2080,128]{1,0:T(8,128)(2,1)S(1)} %shard_map.67), channel_id=1, source_target_pairs={{2,6},{4,0},{6,10},{8,4},{10,14},{12,8},{14,18},{16,12},{18,22},{2... | collective-permute-start | bytes 1597448 | tf_op jit(solution)/shard_map/ppermute | solution.py:303
  32.3 23.0 %collective-permute-start.4 = (s16[2080,128]{1,0:T(8,128)(2,1)S(1)}, s16[2080,128]{1,0:T(8,128)(2,1)S(1)}, u32[]{:S(2)}, u32[]{:S(2)}) collective-permute-start(s16[2080,128]{1,0:T(8,128)(2,1)S(1)} %shard_map.68), channel_id=1, source_target_pairs={{2,4},{4,2},{6,8},{8,6},{10,12},{12,10},{14,16},{16,14},{18,20},{2... | collective-permute-start | bytes 1597448 | tf_op jit(solution)/shard_map/ppermute | solution.py:303
  42.3 6.0 %collective-permute-start.5 = (s16[1040,128]{1,0:T(8,128)(2,1)S(1)}, s16[1040,128]{1,0:T(8,128)(2,1)S(1)}, u32[]{:S(2)}, u32[]{:S(2)}) collective-permute-start(s16[1040,128]{1,0:T(8,128)(2,1)S(1)} %get-tuple-element.45), channel_id=1, source_target_pairs={{0,2},{2,0},{4,6},{6,4},{8,10},{10,8},{12,14},{14,12},{16,18},{18,... | collective-permute-start | bytes 798728 | tf_op jit(solution)/shard_map/ppermute | solution.py:303
  42.4 6.0 %collective-permute-start.6 = (s16[1040,128]{1,0:T(8,128)(2,1)S(1)}, s16[1040,128]{1,0:T(8,128)(2,1)S(1)}, u32[]{:S(2)}, u32[]{:S(2)}) collective-permute-start(s16[1040,128]{1,0:T(8,128)(2,1)S(1)} %get-tuple-element.46), channel_id=1, source_target_pairs={{0,2},{2,0},{4,6},{6,4},{8,10},{10,8},{12,14},{14,12},{16,18},{18,... | collective-permute-start | bytes 798728 | tf_op jit(solution)/shard_map/ppermute | solution.py:303

commit v3 on v2

--- a/solution.py
+++ b/solution.py
@@ -13,10 +13,10 @@
 GROUP = 64
 TOP = 32767.0
 STEPS = 8.0
-LIMIT = 50 * 1024 * 1024
+LIMIT = 43 * 1024 * 1024
 SMEM = pl.BlockSpec(memory_space=pltpu.SMEM)
 VMEM = pl.BlockSpec(memory_space=pltpu.VMEM)
-HBM = pl.BlockSpec(memory_space=pl.ANY)
+HBM = pl.BlockSpec(memory_space=pltpu.HBM)
 
 FAR, IN2, NEAR, IN1, OWN = range(5)
 REACH = (2, -2, 1, -1, 0)
@@ -91,7 +91,7 @@
 def first_kernel(
     shift, counts, rows, voxels, res, tiles, *rest, gates, bins, slots
 ):
-    *parts, sino, far_slots, far_rows, far_counts, raw, acc, buf, near_slots, raw_sem, sems = rest
+    *parts, sino, buf, far_slots, far_rows, far_counts, raw, acc, near_slots, raw_sem, sems = rest
     local_rows = res.shape[0]
     per = slots // CHUNKS
     lead = bins // 2 * gates
@@ -148,19 +148,25 @@
     counts, rows, voxels, far_slots, far_rows, far_counts, sino, tiles, *rest,
     role, gates, bins, slots, send, starts, gots, local_rows
 ):
-    first, got, (*out, acc, buf, sems) = rest[:starts], rest[starts:starts + gots], rest[starts + gots:]
+    first, got, rest = rest[:starts], rest[starts:starts + gots], rest[starts + gots:]
     which = list_of(role)
     count = counts[which]
     per = slots // CHUNKS
     lead = bins // 2 * gates
     span = VT * gates
 
+    if role < SPLIT:
+        *out, acc = rest
+        buf = tiles.at[role]
+    else:
+        *out, acc, buf, sems = rest
+
     def chunk_copy(c):
         return pltpu.make_async_copy(
             tiles.at[which, pl.ds(c * per, per)], buf.at[pl.ds(c * per, per)], sems.at[c]
         )
 
-    for c in range(CHUNKS):
+    for c in range(CHUNKS if role >= SPLIT else 0):
         @pl.when(c * per < count)
         def _():
             chunk_copy(c).start()
@@ -174,15 +180,14 @@
     for i, piece in enumerate(got):
         size = span // gots
         acc[lead + i * size:lead + (i + 1) * size] += widen(piece)
-    for c in range(CHUNKS):
+    for c in range(CHUNKS if role >= SPLIT else 0):
         @pl.when(c * per < count)
         def _():
             chunk_copy(c).wait()
-            if role >= SPLIT:
-                add_slots(
-                    acc, buf, sino, lambda k: k, lambda k, j: place_of(rows[which, j], local_rows),
-                    lambda j: voxels[which, j], c * per, jnp.minimum(count, (c + 1) * per), gates, bins,
-                )
+            add_slots(
+                acc, buf, sino, lambda k: k, lambda k, j: place_of(rows[which, j], local_rows),
+                lambda j: voxels[which, j], c * per, jnp.minimum(count, (c + 1) * per), gates, bins,
+            )
     if role < SPLIT:
         add_slots(
             acc, buf, sino, lambda k: far_slots[role, k], lambda k, j: far_rows[role, k],
@@ -245,17 +250,17 @@
     acc = pltpu.VMEM((span + bins * gates + size, width), jnp.float32)
     image = jax.ShapeDtypeStruct((span, width), jnp.float32)
     table = jax.ShapeDtypeStruct((SPLIT, slots), jnp.int32)
-    *parts, mine, far_slots, far_rows, far_counts = pl.pallas_call(
+    *parts, mine, held_tiles, far_slots, far_rows, far_counts = pl.pallas_call(
         partial(first_kernel, gates=gates, bins=bins, slots=slots),
         out_shape=[image] * SPLIT
         + [jax.ShapeDtypeStruct(res.shape, res.dtype)]
+        + [jax.ShapeDtypeStruct((SPLIT, slots, depth, width), tiles.dtype)]
         + [table, table, jax.ShapeDtypeStruct((SPLIT,), jnp.int32)],
         in_specs=[SMEM] * 4 + [HBM, HBM],
-        out_specs=[VMEM] * (SPLIT + 1) + [SMEM] * 3,
+        out_specs=[VMEM] * (SPLIT + 2) + [SMEM] * 3,
         scratch_shapes=[
             pltpu.VMEM(res.shape, res.dtype),
             acc,
-            pltpu.VMEM((SPLIT, slots, depth, width), jnp.bfloat16),
             pltpu.SMEM((slots,), jnp.int32),
             pltpu.SemaphoreType.DMA(()),
             pltpu.SemaphoreType.DMA((SPLIT, CHUNKS)),
@@ -287,16 +292,19 @@
                 starts=len(starts), gots=len(got), local_rows=local_rows,
             ),
             out_shape=[shape] * pieces if pieces else [image],
-            in_specs=[SMEM] * 6 + [VMEM, HBM] + [VMEM] * (len(starts) + len(got)),
+            in_specs=[SMEM] * 6 + [VMEM, VMEM if role < SPLIT else HBM] + [VMEM] * (len(starts) + len(got)),
             out_specs=[VMEM] * max(pieces, 1),
-            scratch_shapes=[
+            scratch_shapes=[acc]
+            if role < SPLIT
+            else [
                 acc,
                 pltpu.VMEM((slots, depth, width), jnp.bfloat16),
                 pltpu.SemaphoreType.DMA((CHUNKS,)),
             ],
             compiler_params=params,
             cost_estimate=COST,
-        )(held, rows, voxels, far_slots, far_rows, far_counts, sino, tiles, *starts, *got)
+        )(held, rows, voxels, far_slots, far_rows, far_counts, sino,
+          held_tiles if role < SPLIT else tiles, *starts, *got)
         return out, after
 
     def pass_on(sent, route):

time: 57.4 us -> 54.3 us (0.946)
  Pallas kernels: 31.8 us -> 25 us
  waiting for transfers between devices: 11.2 us -> 15.3 us
    pallas_call x5, Pallas kernels: 21.2 us -> 13.8 us  [run(): pl.pallas_call(partial(rest_kernel, role=role, gates=gates, bins=bins, sl...]
    ppermute x6, waiting for transfers between devices: 6.89 us -> 11.6 us  [pass_on(): return [lax.ppermute(piece, 'slab', route) for piece in sent]]
    pallas_call x1, Pallas kernels: 7.19 us -> 7.85 us  [local(): pl.pallas_call(partial(first_kernel, gates=gates, bins=bins, slots=slots)...]
    ppermute x1, waiting for transfers between devices: 4.31 us -> 3.64 us  [local(): lax.ppermute(res, 'blk', [(i, (i + hop) % blocks) for i in range(blocks)])]
    unnamed x9 -> x7, local copies, waits for them, and re-layouts: 3.1 us -> 3.1 us
  transfers between devices with their start and end apart: 7 -> 7, of which waited for: 2 -> 3; matrix products, arithmetic and copies ran while one was open for 1% -> 1% of each run, Pallas kernels for 45% -> 36%
where the time goes in v3:
time: 54.3 us; the launch traced here: 53.9 us
  Pallas kernels  25 us (46%)
  waiting for transfers between devices  15.3 us (28%)
  starting transfers between devices  10.4 us (19%)
  local copies, waits for them, and re-layouts  3.1 us (6%)
    pallas_call x5, Pallas kernels, run(): pl.pallas_call(partial(rest_kernel, role=role, gates=gates, bins=bins, sl...  13.8 us
    ppermute x6, waiting for transfers between devices, pass_on(): return [lax.ppermute(piece, 'slab', route) for piece in sent]  11.6 us
    ppermute x6, starting transfers between devices, pass_on(): return [lax.ppermute(piece, 'slab', route) for piece in sent]  9.17 us
    pallas_call x1, Pallas kernels, local(): pl.pallas_call(partial(first_kernel, gates=gates, bins=bins, slots=slots)...  7.85 us
    ppermute x1, waiting for transfers between devices, local(): lax.ppermute(res, 'blk', [(i, (i + hop) % blocks) for i in range(blocks)])  3.64 us
    unnamed x7, local copies, waits for them, and re-layouts  3.1 us
    pallas_call x1, Pallas kernels, local(): pl.pallas_call(join_image, out_shape=image, in_specs=[VMEM] * (3 + PIECES...  1.88 us
    pallas_call x1, Pallas kernels, local(): pl.pallas_call(partial(join_kernel, gates=gates, bins=bins), out_shape=ja...  1.47 us
  transfers between devices with their start and end apart: 7, of which 3 were waited for; matrix products, arithmetic and copies ran while one was open for 1% of the time, Pallas kernels for 36%

profile of v3, /device:TPU:9, one launch (start us, length us, event | category | flops | bytes accessed | tf_op | source)
XLA Modules:
  0.0 53.9 jit_solution(6283292701268760815)
XLA Ops:
  0.0 1.2 %collective-permute-start = (bf16[8,320,128]{2,1,0:T(8,128)(2,1)}, bf16[8,320,128]{2,1,0:T(8,128)(2,1)S(1)}, u32[]{:S(2)}, u32[]{:S(2)}) collective-permute-start(bf16[8,320,128]{2,1,0:T(8,128)(2,1)} %bitcast.8), channel_id=1, source_target_pairs={{0,1},{1,0},{2,3},{3,2},{4,5},{5,4},{6,7},{7,6},{8,9},{9,8},{10,11... | collective-permute-start | bytes 1966088 | tf_op jit(solution)/shard_map/ppermute | solution.py:245
  1.2 0.7 %copy_bitcast_fusion = (s32[5,64]{1,0:T(8,128)S(1)}, s32[5,64]{1,0:T(8,128)S(1)}) fusion(s32[1,1,5,64]{3,1,2,0:T(1,128)} %param.9, s32[1,1,5,64]{3,1,2,0:T(1,128)} %param.8), kind=kLoop, calls=%fused_computation | loop fusion | bytes 5120
  1.9 0.0 copy-start
  1.9 1.1 %copy-done = bf16[1,8,8,40,128]{4,3,2,1,0:T(8,128)(2,1)S(1)} copy-done((bf16[1,8,8,40,128]{4,3,2,1,0:T(8,128)(2,1)S(1)}, bf16[1,8,8,40,128]{4,3,2,1,0:T(8,128)(2,1)}, u32[]{:S(2)}) %copy-start) | copy-done | bytes 655384
  3.0 0.0 copy-start.1
  3.0 0.7 %copy-done.1 = s32[1,1,5]{2,1,0:T(1,128)S(1)} copy-done((s32[1,1,5]{2,1,0:T(1,128)S(1)}, s32[1,1,5]{2,1,0:T(1,128)}, u32[]{:S(2)}) %copy-start.1) | copy-done | bytes 44
  3.7 0.0 copy-start.2
  3.7 0.7 %copy-done.2 = s32[40]{0:T(128)S(1)} copy-done((s32[40]{0:T(128)S(1)}, s32[40]{0:T(128)}, u32[]{:S(2)}) %copy-start.2) | copy-done | bytes 184
  4.3 7.9 %shard_map.64 = (f32[2048,128]{1,0:T(8,128)S(1)}, f32[2048,128]{1,0:T(8,128)S(1)}, f32[2048,128]{1,0:T(8,128)S(1)}, bf16[8,320,128]{2,1,0:T(8,128)(2,1)S(1)}, bf...) custom-call(s32[40]{0:T(128)S(1)} %copy-done.2, ...), custom_call_target="tpu_custom_call" | custom-call | flops 1000 | bytes 1000 | tf_op jit(solution)/shard_map/pallas_call | solution.py:253
  12.2 3.6 %collective-permute-done.others = bf16[8,320,128]{2,1,0:T(8,128)(2,1)S(1)} collective-permute-done((bf16[8,320,128]{2,1,0:T(8,128)(2,1)}, bf16[8,320,128]{2,1,0:T(8,128)(2,1)S(1)}, u32[]{:S(2)}, u32[]{:S(2)}) %collective-permute-start) | collective-permute-done | bytes 655392 | tf_op jit(solution)/shard_map/ppermute | solution.py:245
  15.8 1.5 %shard_map.65.sino = bf16[16,320,128]{2,1,0:T(8,128)(2,1)S(1)} custom-call(s32[40]{0:T(128)S(1)} %copy-done.2, bf16[8,320,128]{2,1,0:T(8,128)(2,1)S(1)} %get-tuple-element.30.mine, bf16[8,320,128]{2,1,0:T(8,128)(2,1)S(1)} %collective-permute-done.others), custom_call_target="tpu_custom_call" | custom-call | flops 1000 | bytes 1000 | tf_op jit(solution)/shard_map/pallas_call | solution.py:272
  17.3 2.3 %shard_map.66 = (s16[1040,128]{1,0:T(8,128)(2,1)S(1)}, s16[1040,128]{1,0:T(8,128)(2,1)S(1)}) custom-call(s32[5]{0:T(128)S(1)} %bitcast.11, s32[5,64]{1,0:T(8,128)S(1)} %get-tuple-element.50.rows, s32[5,64]{1,0:T(8,128)S(1)} %get-tuple-element.49.voxels, s32[3,64]{1,0:T(4,128)S(1)} %get-tuple-element.27.far_slots, s32[3,64]{1,0:T(4,128)S(1)} %get-tuple-element.28.far_rows, ...), custom_call_target="tpu_custom_call" | custom-call | flops 1000 | bytes 1000 | tf_op jit(solution)/shard_map/pallas_call | solution.py:289
  19.6 2.4 %collective-permute-start.1 = (s16[1040,128]{1,0:T(8,128)(2,1)S(1)}, s16[1040,128]{1,0:T(8,128)(2,1)S(1)}, u32[]{:S(2)}, u32[]{:S(2)}) collective-permute-start(s16[1040,128]{1,0:T(8,128)(2,1)S(1)} %get-tuple-element.39), channel_id=1, source_target_pairs={{0,2},{2,0},{4,6},{6,4},{8,10},{10,8},{12,14},{14,12},{16,18},{18,... | collective-permute-start | bytes 798728 | tf_op jit(solution)/shard_map/ppermute | solution.py:311
  22.0 0.1 collective-permute-start.2
  22.1 1.8 %shard_map.67 = s16[2080,128]{1,0:T(8,128)(2,1)S(1)} custom-call(s32[5]{0:T(128)S(1)} %bitcast.12, s32[5,64]{1,0:T(8,128)S(1)} %get-tuple-element.50.rows, s32[5,64]{1,0:T(8,128)S(1)} %get-tuple-element.49.voxels, s32[3,64]{1,0:T(4,128)S(1)} %get-tuple-element.27.far_slots, s32[3,64]{1,0:T(4,128)S(1)} %get-tuple-element.28.far_rows, ...), custom_call_target="tpu_custom_call" | custom-call | flops 1000 | bytes 1000 | tf_op jit(solution)/shard_map/pallas_call | solution.py:289
  23.9 3.9 %collective-permute-start.3 = (s16[2080,128]{1,0:T(8,128)(2,1)S(1)}, s16[2080,128]{1,0:T(8,128)(2,1)S(1)}, u32[]{:S(2)}, u32[]{:S(2)}) collective-permute-start(s16[2080,128]{1,0:T(8,128)(2,1)S(1)} %shard_map.67), channel_id=1, source_target_pairs={{2,6},{4,0},{6,10},{8,4},{10,14},{12,8},{14,18},{16,12},{18,22},{2... | collective-permute-start | bytes 1597448 | tf_op jit(solution)/shard_map/ppermute | solution.py:311
  27.8 0.0 collective-permute-done.1.rest_1_
  27.9 0.0 collective-permute-done.2.rest_2_
  27.9 2.8 %shard_map.68 = s16[2080,128]{1,0:T(8,128)(2,1)S(1)} custom-call(s32[5]{0:T(128)S(1)} %bitcast.13, s32[5,64]{1,0:T(8,128)S(1)} %get-tuple-element.50.rows, s32[5,64]{1,0:T(8,128)S(1)} %get-tuple-element.49.voxels, s32[3,64]{1,0:T(4,128)S(1)} %get-tuple-element.27.far_slots, s32[3,64]{1,0:T(4,128)S(1)} %get-tuple-element.28.far_rows, ...), custom_call_target="tpu_custom_call" | custom-call | flops 1000 | bytes 1000 | tf_op jit(solution)/shard_map/pallas_call | solution.py:289
  30.7 2.2 %collective-permute-start.4 = (s16[2080,128]{1,0:T(8,128)(2,1)S(1)}, s16[2080,128]{1,0:T(8,128)(2,1)S(1)}, u32[]{:S(2)}, u32[]{:S(2)}) collective-permute-start(s16[2080,128]{1,0:T(8,128)(2,1)S(1)} %shard_map.68), channel_id=1, source_target_pairs={{2,4},{4,2},{6,8},{8,6},{10,12},{12,10},{14,16},{16,14},{18,20},{2... | collective-permute-start | bytes 1597448 | tf_op jit(solution)/shard_map/ppermute | solution.py:311
  32.9 3.6 %shard_map.69 = (s16[1040,128]{1,0:T(8,128)(2,1)S(1)}, s16[1040,128]{1,0:T(8,128)(2,1)S(1)}) custom-call(s32[5]{0:T(128)S(1)} %bitcast.14, s32[5,64]{1,0:T(8,128)S(1)} %get-tuple-element.50.rows, s32[5,64]{1,0:T(8,128)S(1)} %get-tuple-element.49.voxels, s32[3,64]{1,0:T(4,128)S(1)} %get-tuple-element.27.far_slots, s32[3,64]{1,0:T(4,128)S(1)} %get-tuple-element.28.far_rows, ...), custom_call_target="tpu_custom_call" | custom-call | flops 1000 | bytes 1000 | tf_op jit(solution)/shard_map/pallas_call | solution.py:289
  36.5 0.5 collective-permute-start.5
  37.1 0.1 collective-permute-start.6
  37.1 3.2 %shard_map.70.own = f32[2048,128]{1,0:T(8,128)S(1)} custom-call(s32[5]{0:T(128)S(1)} %bitcast.15, s32[5,64]{1,0:T(8,128)S(1)} %get-tuple-element.50.rows, s32[5,64]{1,0:T(8,128)S(1)} %get-tuple-element.49.voxels, s32[3,64]{1,0:T(4,128)S(1)} %get-tuple-element.27.far_slots, s32[3,64]{1,0:T(4,128)S(1)} %get-tuple-element.28.far_rows, ...), custom_call_target="tpu_custom_call" | custom-call | flops 1000 | bytes 1000 | tf_op jit(solution)/shard_map/pallas_call | solution.py:289
  40.3 0.0 collective-permute-done.5.rest_0_
  40.3 0.0 collective-permute-done.6.rest_1_
  40.3 5.1 %collective-permute-done.3.far = s16[2080,128]{1,0:T(8,128)(2,1)S(1)} collective-permute-done((s16[2080,128]{1,0:T(8,128)(2,1)S(1)}, s16[2080,128]{1,0:T(8,128)(2,1)S(1)}, u32[]{:S(2)}, u32[]{:S(2)}) %collective-permute-start.3) | collective-permute-done | bytes 532512 | tf_op jit(solution)/shard_map/ppermute | solution.py:311
  45.5 6.5 %collective-permute-done.4.near = s16[2080,128]{1,0:T(8,128)(2,1)S(1)} collective-permute-done((s16[2080,128]{1,0:T(8,128)(2,1)S(1)}, s16[2080,128]{1,0:T(8,128)(2,1)S(1)}, u32[]{:S(2)}, u32[]{:S(2)}) %collective-permute-start.4) | collective-permute-done | bytes 532512 | tf_op jit(solution)/shard_map/ppermute | solution.py:311
  52.0 1.9 %shard_map.71 = f32[2048,128]{1,0:T(8,128)} custom-call(f32[2048,128]{1,0:T(8,128)S(1)} %shard_map.70.own, s16[2080,128]{1,0:T(8,128)(2,1)S(1)} %collective-permute-done.3.far, s16[2080,128]{1,0:T(8,128)(2,1)S(1)} %collective-permute-done.4.near, s16[1040,128]{1,0:T(8,128)(2,1)S(1)} %collective-permute-done.5.rest_0_, ...), custom_call_target="tpu_custom_call" | custom-call | flops 1000 | bytes 1000 | tf_op jit(solution)/shard_map/pallas_call | solution.py:331
Async XLA Ops:
  0.0 15.8 %collective-permute-start = (bf16[8,320,128]{2,1,0:T(8,128)(2,1)}, bf16[8,320,128]{2,1,0:T(8,128)(2,1)S(1)}, u32[]{:S(2)}, u32[]{:S(2)}) collective-permute-start(bf16[8,320,128]{2,1,0:T(8,128)(2,1)} %bitcast.8), channel_id=1, source_target_pairs={{0,1},{1,0},{2,3},{3,2},{4,5},{5,4},{6,7},{7,6},{8,9},{9,8},{10,11... | collective-permute-start | bytes 1966088 | tf_op jit(solution)/shard_map/ppermute | solution.py:245
  1.9 1.1 %copy-start = (bf16[1,8,8,40,128]{4,3,2,1,0:T(8,128)(2,1)S(1)}, bf16[1,8,8,40,128]{4,3,2,1,0:T(8,128)(2,1)}, u32[]{:S(2)}) copy-start(bf16[1,8,8,40,128]{4,3,2,1,0:T(8,128)(2,1)} %param.6) | copy-start | bytes 1966084
  3.0 0.7 %copy-start.1 = (s32[1,1,5]{2,1,0:T(1,128)S(1)}, s32[1,1,5]{2,1,0:T(1,128)}, u32[]{:S(2)}) copy-start(s32[1,1,5]{2,1,0:T(1,128)} %param.10) | copy-start | bytes 64
  3.7 0.7 %copy-start.2 = (s32[40]{0:T(128)S(1)}, s32[40]{0:T(128)}, u32[]{:S(2)}) copy-start(s32[40]{0:T(128)} %shift.3) | copy-start | bytes 484
  19.6 8.2 %collective-permute-start.1 = (s16[1040,128]{1,0:T(8,128)(2,1)S(1)}, s16[1040,128]{1,0:T(8,128)(2,1)S(1)}, u32[]{:S(2)}, u32[]{:S(2)}) collective-permute-start(s16[1040,128]{1,0:T(8,128)(2,1)S(1)} %get-tuple-element.39), channel_id=1, source_target_pairs={{0,2},{2,0},{4,6},{6,4},{8,10},{10,8},{12,14},{14,12},{16,18},{18,... | collective-permute-start | bytes 798728 | tf_op jit(solution)/shard_map/ppermute | solution.py:311
  22.0 5.9 %collective-permute-start.2 = (s16[1040,128]{1,0:T(8,128)(2,1)S(1)}, s16[1040,128]{1,0:T(8,128)(2,1)S(1)}, u32[]{:S(2)}, u32[]{:S(2)}) collective-permute-start(s16[1040,128]{1,0:T(8,128)(2,1)S(1)} %get-tuple-element.40), channel_id=1, source_target_pairs={{0,2},{2,0},{4,6},{6,4},{8,10},{10,8},{12,14},{14,12},{16,18},{18,... | collective-permute-start | bytes 798728 | tf_op jit(solution)/shard_map/ppermute | solution.py:311
  23.9 21.5 %collective-permute-start.3 = (s16[2080,128]{1,0:T(8,128)(2,1)S(1)}, s16[2080,128]{1,0:T(8,128)(2,1)S(1)}, u32[]{:S(2)}, u32[]{:S(2)}) collective-permute-start(s16[2080,128]{1,0:T(8,128)(2,1)S(1)} %shard_map.67), channel_id=1, source_target_pairs={{2,6},{4,0},{6,10},{8,4},{10,14},{12,8},{14,18},{16,12},{18,22},{2... | collective-permute-start | bytes 1597448 | tf_op jit(solution)/shard_map/ppermute | solution.py:311
  30.7 21.3 %collective-permute-start.4 = (s16[2080,128]{1,0:T(8,128)(2,1)S(1)}, s16[2080,128]{1,0:T(8,128)(2,1)S(1)}, u32[]{:S(2)}, u32[]{:S(2)}) collective-permute-start(s16[2080,128]{1,0:T(8,128)(2,1)S(1)} %shard_map.68), channel_id=1, source_target_pairs={{2,4},{4,2},{6,8},{8,6},{10,12},{12,10},{14,16},{16,14},{18,20},{2... | collective-permute-start | bytes 1597448 | tf_op jit(solution)/shard_map/ppermute | solution.py:311
  36.5 3.8 %collective-permute-start.5 = (s16[1040,128]{1,0:T(8,128)(2,1)S(1)}, s16[1040,128]{1,0:T(8,128)(2,1)S(1)}, u32[]{:S(2)}, u32[]{:S(2)}) collective-permute-start(s16[1040,128]{1,0:T(8,128)(2,1)S(1)} %get-tuple-element.47), channel_id=1, source_target_pairs={{0,2},{2,0},{4,6},{6,4},{8,10},{10,8},{12,14},{14,12},{16,18},{18,... | collective-permute-start | bytes 798728 | tf_op jit(solution)/shard_map/ppermute | solution.py:311
  37.1 3.3 %collective-permute-start.6 = (s16[1040,128]{1,0:T(8,128)(2,1)S(1)}, s16[1040,128]{1,0:T(8,128)(2,1)S(1)}, u32[]{:S(2)}, u32[]{:S(2)}) collective-permute-start(s16[1040,128]{1,0:T(8,128)(2,1)S(1)} %get-tuple-element.48), channel_id=1, source_target_pairs={{0,2},{2,0},{4,6},{6,4},{8,10},{10,8},{12,14},{14,12},{16,18},{18,... | collective-permute-start | bytes 798728 | tf_op jit(solution)/shard_map/ppermute | solution.py:311

commit v4 on v3

--- a/solution.py
+++ b/solution.py
@@ -31,18 +31,14 @@
 
     def group(i, carry):
         first = begin + i * UNROLL
-        outs = []
-        ats = []
         for u in range(UNROLL):
             k = first + u
             live = k < total
             j = jnp.where(live, slot_of(k), 0)
             row = jnp.where(live, row_of(k, j), 0)
             v = jnp.where(live, voxel_of(j), dump)
-            ats.append(pl.ds(pl.multiple_of(v * gates, gates), size))
-            outs.append(jnp.dot(sino[row], buf[j], preferred_element_type=jnp.float32))
-        for at, out in zip(ats, outs):
-            acc[at] += out
+            at = pl.ds(pl.multiple_of(v * gates, gates), size)
+            acc[at] += jnp.dot(sino[row], buf[j], preferred_element_type=jnp.float32)
         return carry
 
     lax.fori_loop(0, (total - begin + UNROLL - 1) // UNROLL, group, 0)

time: 54.3 us -> 54.6 us (level)
  waiting for transfers between devices: 15.3 us -> 10.5 us
  Pallas kernels: 25 us -> 28.5 us
  starting transfers between devices: 10.4 us -> 11.9 us
    ppermute x6, waiting for transfers between devices: 11.6 us -> 6.82 us  [pass_on(): return [lax.ppermute(piece, 'slab', route) for piece in sent]]
    pallas_call x5, Pallas kernels: 13.8 us -> 17.3 us  [run(): pl.pallas_call(partial(rest_kernel, role=role, gates=gates, bins=bins, sl...]
    ppermute x6, starting transfers between devices: 9.17 us -> 10.7 us  [pass_on(): return [lax.ppermute(piece, 'slab', route) for piece in sent]]
  transfers between devices with their start and end apart: 7 -> 7, of which waited for: 3 -> 2; matrix products, arithmetic and copies ran while one was open for 1% -> 1% of each run, Pallas kernels for 36% -> 43%
where the time goes in v4:
time: 54.6 us; the launch traced here: 54.1 us
  Pallas kernels  28.5 us (52%)
  starting transfers between devices  11.9 us (22%)
  waiting for transfers between devices  10.5 us (19%)
  local copies, waits for them, and re-layouts  3.1 us (6%)
    pallas_call x5, Pallas kernels, run(): pl.pallas_call(partial(rest_kernel, role=role, gates=gates, bins=bins, sl...  17.3 us
    ppermute x6, starting transfers between devices, pass_on(): return [lax.ppermute(piece, 'slab', route) for piece in sent]  10.7 us
    pallas_call x1, Pallas kernels, local(): pl.pallas_call(partial(first_kernel, gates=gates, bins=bins, slots=slots)...  7.79 us
    ppermute x6, waiting for transfers between devices, pass_on(): return [lax.ppermute(piece, 'slab', route) for piece in sent]  6.82 us
    ppermute x1, waiting for transfers between devices, local(): lax.ppermute(res, 'blk', [(i, (i + hop) % blocks) for i in range(blocks)])  3.7 us
    unnamed x7, local copies, waits for them, and re-layouts  3.1 us
    pallas_call x1, Pallas kernels, local(): pl.pallas_call(join_image, out_shape=image, in_specs=[VMEM] * (3 + PIECES...  1.88 us
    pallas_call x1, Pallas kernels, local(): pl.pallas_call(partial(join_kernel, gates=gates, bins=bins), out_shape=ja...  1.47 us
  transfers between devices with their start and end apart: 7, of which 2 were waited for; matrix products, arithmetic and copies ran while one was open for 1% of the time, Pallas kernels for 43%

profile of v4, /device:TPU:9, one launch (start us, length us, event | category | flops | bytes accessed | tf_op | source)
XLA Modules:
  0.0 54.1 jit_solution(11685824347489031993)
XLA Ops:
  0.0 1.2 %collective-permute-start = (bf16[8,320,128]{2,1,0:T(8,128)(2,1)}, bf16[8,320,128]{2,1,0:T(8,128)(2,1)S(1)}, u32[]{:S(2)}, u32[]{:S(2)}) collective-permute-start(bf16[8,320,128]{2,1,0:T(8,128)(2,1)} %bitcast.8), channel_id=1, source_target_pairs={{0,1},{1,0},{2,3},{3,2},{4,5},{5,4},{6,7},{7,6},{8,9},{9,8},{10,11... | collective-permute-start | bytes 1966088 | tf_op jit(solution)/shard_map/ppermute | solution.py:241
  1.2 0.7 %copy_bitcast_fusion = (s32[5,64]{1,0:T(8,128)S(1)}, s32[5,64]{1,0:T(8,128)S(1)}) fusion(s32[1,1,5,64]{3,1,2,0:T(1,128)} %param.9, s32[1,1,5,64]{3,1,2,0:T(1,128)} %param.8), kind=kLoop, calls=%fused_computation | loop fusion | bytes 5120
  1.9 0.0 copy-start
  1.9 1.1 %copy-done = bf16[1,8,8,40,128]{4,3,2,1,0:T(8,128)(2,1)S(1)} copy-done((bf16[1,8,8,40,128]{4,3,2,1,0:T(8,128)(2,1)S(1)}, bf16[1,8,8,40,128]{4,3,2,1,0:T(8,128)(2,1)}, u32[]{:S(2)}) %copy-start) | copy-done | bytes 655384
  3.0 0.0 copy-start.1
  3.0 0.7 %copy-done.1 = s32[1,1,5]{2,1,0:T(1,128)S(1)} copy-done((s32[1,1,5]{2,1,0:T(1,128)S(1)}, s32[1,1,5]{2,1,0:T(1,128)}, u32[]{:S(2)}) %copy-start.1) | copy-done | bytes 44
  3.7 0.0 copy-start.2
  3.7 0.7 %copy-done.2 = s32[40]{0:T(128)S(1)} copy-done((s32[40]{0:T(128)S(1)}, s32[40]{0:T(128)}, u32[]{:S(2)}) %copy-start.2) | copy-done | bytes 184
  4.3 7.8 %shard_map.64 = (f32[2048,128]{1,0:T(8,128)S(1)}, f32[2048,128]{1,0:T(8,128)S(1)}, f32[2048,128]{1,0:T(8,128)S(1)}, bf16[8,320,128]{2,1,0:T(8,128)(2,1)S(1)}, bf...) custom-call(s32[40]{0:T(128)S(1)} %copy-done.2, ...), custom_call_target="tpu_custom_call" | custom-call | flops 1000 | bytes 1000 | tf_op jit(solution)/shard_map/pallas_call | solution.py:249
  12.1 3.7 %collective-permute-done.others = bf16[8,320,128]{2,1,0:T(8,128)(2,1)S(1)} collective-permute-done((bf16[8,320,128]{2,1,0:T(8,128)(2,1)}, bf16[8,320,128]{2,1,0:T(8,128)(2,1)S(1)}, u32[]{:S(2)}, u32[]{:S(2)}) %collective-permute-start) | collective-permute-done | bytes 655392 | tf_op jit(solution)/shard_map/ppermute | solution.py:241
  15.8 1.5 %shard_map.65.sino = bf16[16,320,128]{2,1,0:T(8,128)(2,1)S(1)} custom-call(s32[40]{0:T(128)S(1)} %copy-done.2, bf16[8,320,128]{2,1,0:T(8,128)(2,1)S(1)} %get-tuple-element.30.mine, bf16[8,320,128]{2,1,0:T(8,128)(2,1)S(1)} %collective-permute-done.others), custom_call_target="tpu_custom_call" | custom-call | flops 1000 | bytes 1000 | tf_op jit(solution)/shard_map/pallas_call | solution.py:268
  17.3 1.6 %shard_map.66 = (s16[1040,128]{1,0:T(8,128)(2,1)S(1)}, s16[1040,128]{1,0:T(8,128)(2,1)S(1)}) custom-call(s32[5]{0:T(128)S(1)} %bitcast.11, s32[5,64]{1,0:T(8,128)S(1)} %get-tuple-element.50.rows, s32[5,64]{1,0:T(8,128)S(1)} %get-tuple-element.49.voxels, s32[3,64]{1,0:T(4,128)S(1)} %get-tuple-element.27.far_slots, s32[3,64]{1,0:T(4,128)S(1)} %get-tuple-element.28.far_rows, ...), custom_call_target="tpu_custom_call" | custom-call | flops 1000 | bytes 1000 | tf_op jit(solution)/shard_map/pallas_call | solution.py:285
  18.9 2.9 %collective-permute-start.1 = (s16[1040,128]{1,0:T(8,128)(2,1)S(1)}, s16[1040,128]{1,0:T(8,128)(2,1)S(1)}, u32[]{:S(2)}, u32[]{:S(2)}) collective-permute-start(s16[1040,128]{1,0:T(8,128)(2,1)S(1)} %get-tuple-element.39), channel_id=1, source_target_pairs={{0,2},{2,0},{4,6},{6,4},{8,10},{10,8},{12,14},{14,12},{16,18},{18,... | collective-permute-start | bytes 798728 | tf_op jit(solution)/shard_map/ppermute | solution.py:307
  21.8 0.1 collective-permute-start.2
  21.8 2.3 %shard_map.67 = s16[2080,128]{1,0:T(8,128)(2,1)S(1)} custom-call(s32[5]{0:T(128)S(1)} %bitcast.12, s32[5,64]{1,0:T(8,128)S(1)} %get-tuple-element.50.rows, s32[5,64]{1,0:T(8,128)S(1)} %get-tuple-element.49.voxels, s32[3,64]{1,0:T(4,128)S(1)} %get-tuple-element.27.far_slots, s32[3,64]{1,0:T(4,128)S(1)} %get-tuple-element.28.far_rows, ...), custom_call_target="tpu_custom_call" | custom-call | flops 1000 | bytes 1000 | tf_op jit(solution)/shard_map/pallas_call | solution.py:285
  24.2 3.1 %collective-permute-start.3 = (s16[2080,128]{1,0:T(8,128)(2,1)S(1)}, s16[2080,128]{1,0:T(8,128)(2,1)S(1)}, u32[]{:S(2)}, u32[]{:S(2)}) collective-permute-start(s16[2080,128]{1,0:T(8,128)(2,1)S(1)} %shard_map.67), channel_id=1, source_target_pairs={{2,6},{4,0},{6,10},{8,4},{10,14},{12,8},{14,18},{16,12},{18,22},{2... | collective-permute-start | bytes 1597448 | tf_op jit(solution)/shard_map/ppermute | solution.py:307
  27.3 0.0 collective-permute-done.1.rest_1_
  27.4 0.0 collective-permute-done.2.rest_2_
  27.4 2.6 %shard_map.68 = s16[2080,128]{1,0:T(8,128)(2,1)S(1)} custom-call(s32[5]{0:T(128)S(1)} %bitcast.13, s32[5,64]{1,0:T(8,128)S(1)} %get-tuple-element.50.rows, s32[5,64]{1,0:T(8,128)S(1)} %get-tuple-element.49.voxels, s32[3,64]{1,0:T(4,128)S(1)} %get-tuple-element.27.far_slots, s32[3,64]{1,0:T(4,128)S(1)} %get-tuple-element.28.far_rows, ...), custom_call_target="tpu_custom_call" | custom-call | flops 1000 | bytes 1000 | tf_op jit(solution)/shard_map/pallas_call | solution.py:285
  29.9 4.0 %collective-permute-start.4 = (s16[2080,128]{1,0:T(8,128)(2,1)S(1)}, s16[2080,128]{1,0:T(8,128)(2,1)S(1)}, u32[]{:S(2)}, u32[]{:S(2)}) collective-permute-start(s16[2080,128]{1,0:T(8,128)(2,1)S(1)} %shard_map.68), channel_id=1, source_target_pairs={{2,4},{4,2},{6,8},{8,6},{10,12},{12,10},{14,16},{16,14},{18,20},{2... | collective-permute-start | bytes 1597448 | tf_op jit(solution)/shard_map/ppermute | solution.py:307
  34.0 5.4 %shard_map.69 = (s16[1040,128]{1,0:T(8,128)(2,1)S(1)}, s16[1040,128]{1,0:T(8,128)(2,1)S(1)}) custom-call(s32[5]{0:T(128)S(1)} %bitcast.14, s32[5,64]{1,0:T(8,128)S(1)} %get-tuple-element.50.rows, s32[5,64]{1,0:T(8,128)S(1)} %get-tuple-element.49.voxels, s32[3,64]{1,0:T(4,128)S(1)} %get-tuple-element.27.far_slots, s32[3,64]{1,0:T(4,128)S(1)} %get-tuple-element.28.far_rows, ...), custom_call_target="tpu_custom_call" | custom-call | flops 1000 | bytes 1000 | tf_op jit(solution)/shard_map/pallas_call | solution.py:285
  39.3 0.1 collective-permute-start.5
  39.4 0.5 collective-permute-start.6
  39.9 5.4 %shard_map.70.own = f32[2048,128]{1,0:T(8,128)S(1)} custom-call(s32[5]{0:T(128)S(1)} %bitcast.15, s32[5,64]{1,0:T(8,128)S(1)} %get-tuple-element.50.rows, s32[5,64]{1,0:T(8,128)S(1)} %get-tuple-element.49.voxels, s32[3,64]{1,0:T(4,128)S(1)} %get-tuple-element.27.far_slots, s32[3,64]{1,0:T(4,128)S(1)} %get-tuple-element.28.far_rows, ...), custom_call_target="tpu_custom_call" | custom-call | flops 1000 | bytes 1000 | tf_op jit(solution)/shard_map/pallas_call | solution.py:285
  45.4 0.0 collective-permute-done.5.rest_0_
  45.4 0.0 collective-permute-done.6.rest_1_
  45.4 0.0 collective-permute-done.3.far
  45.4 6.8 %collective-permute-done.4.near = s16[2080,128]{1,0:T(8,128)(2,1)S(1)} collective-permute-done((s16[2080,128]{1,0:T(8,128)(2,1)S(1)}, s16[2080,128]{1,0:T(8,128)(2,1)S(1)}, u32[]{:S(2)}, u32[]{:S(2)}) %collective-permute-start.4) | collective-permute-done | bytes 532512 | tf_op jit(solution)/shard_map/ppermute | solution.py:307
  52.2 1.9 %shard_map.71 = f32[2048,128]{1,0:T(8,128)} custom-call(f32[2048,128]{1,0:T(8,128)S(1)} %shard_map.70.own, s16[2080,128]{1,0:T(8,128)(2,1)S(1)} %collective-permute-done.3.far, s16[2080,128]{1,0:T(8,128)(2,1)S(1)} %collective-permute-done.4.near, s16[1040,128]{1,0:T(8,128)(2,1)S(1)} %collective-permute-done.5.rest_0_, ...), custom_call_target="tpu_custom_call" | custom-call | flops 1000 | bytes 1000 | tf_op jit(solution)/shard_map/pallas_call | solution.py:327
Async XLA Ops:
  0.0 15.8 %collective-permute-start = (bf16[8,320,128]{2,1,0:T(8,128)(2,1)}, bf16[8,320,128]{2,1,0:T(8,128)(2,1)S(1)}, u32[]{:S(2)}, u32[]{:S(2)}) collective-permute-start(bf16[8,320,128]{2,1,0:T(8,128)(2,1)} %bitcast.8), channel_id=1, source_target_pairs={{0,1},{1,0},{2,3},{3,2},{4,5},{5,4},{6,7},{7,6},{8,9},{9,8},{10,11... | collective-permute-start | bytes 1966088 | tf_op jit(solution)/shard_map/ppermute | solution.py:241
  1.9 1.1 %copy-start = (bf16[1,8,8,40,128]{4,3,2,1,0:T(8,128)(2,1)S(1)}, bf16[1,8,8,40,128]{4,3,2,1,0:T(8,128)(2,1)}, u32[]{:S(2)}) copy-start(bf16[1,8,8,40,128]{4,3,2,1,0:T(8,128)(2,1)} %param.6) | copy-start | bytes 1966084
  3.0 0.7 %copy-start.1 = (s32[1,1,5]{2,1,0:T(1,128)S(1)}, s32[1,1,5]{2,1,0:T(1,128)}, u32[]{:S(2)}) copy-start(s32[1,1,5]{2,1,0:T(1,128)} %param.10) | copy-start | bytes 64
  3.7 0.7 %copy-start.2 = (s32[40]{0:T(128)S(1)}, s32[40]{0:T(128)}, u32[]{:S(2)}) copy-start(s32[40]{0:T(128)} %shift.3) | copy-start | bytes 484
  18.9 8.5 %collective-permute-start.1 = (s16[1040,128]{1,0:T(8,128)(2,1)S(1)}, s16[1040,128]{1,0:T(8,128)(2,1)S(1)}, u32[]{:S(2)}, u32[]{:S(2)}) collective-permute-start(s16[1040,128]{1,0:T(8,128)(2,1)S(1)} %get-tuple-element.39), channel_id=1, source_target_pairs={{0,2},{2,0},{4,6},{6,4},{8,10},{10,8},{12,14},{14,12},{16,18},{18,... | collective-permute-start | bytes 798728 | tf_op jit(solution)/shard_map/ppermute | solution.py:307
  21.8 5.6 %collective-permute-start.2 = (s16[1040,128]{1,0:T(8,128)(2,1)S(1)}, s16[1040,128]{1,0:T(8,128)(2,1)S(1)}, u32[]{:S(2)}, u32[]{:S(2)}) collective-permute-start(s16[1040,128]{1,0:T(8,128)(2,1)S(1)} %get-tuple-element.40), channel_id=1, source_target_pairs={{0,2},{2,0},{4,6},{6,4},{8,10},{10,8},{12,14},{14,12},{16,18},{18,... | collective-permute-start | bytes 798728 | tf_op jit(solution)/shard_map/ppermute | solution.py:307
  24.2 21.2 %collective-permute-start.3 = (s16[2080,128]{1,0:T(8,128)(2,1)S(1)}, s16[2080,128]{1,0:T(8,128)(2,1)S(1)}, u32[]{:S(2)}, u32[]{:S(2)}) collective-permute-start(s16[2080,128]{1,0:T(8,128)(2,1)S(1)} %shard_map.67), channel_id=1, source_target_pairs={{2,6},{4,0},{6,10},{8,4},{10,14},{12,8},{14,18},{16,12},{18,22},{2... | collective-permute-start | bytes 1597448 | tf_op jit(solution)/shard_map/ppermute | solution.py:307
  29.9 22.3 %collective-permute-start.4 = (s16[2080,128]{1,0:T(8,128)(2,1)S(1)}, s16[2080,128]{1,0:T(8,128)(2,1)S(1)}, u32[]{:S(2)}, u32[]{:S(2)}) collective-permute-start(s16[2080,128]{1,0:T(8,128)(2,1)S(1)} %shard_map.68), channel_id=1, source_target_pairs={{2,4},{4,2},{6,8},{8,6},{10,12},{12,10},{14,16},{16,14},{18,20},{2... | collective-permute-start | bytes 1597448 | tf_op jit(solution)/shard_map/ppermute | solution.py:307
  39.3 6.0 %collective-permute-start.5 = (s16[1040,128]{1,0:T(8,128)(2,1)S(1)}, s16[1040,128]{1,0:T(8,128)(2,1)S(1)}, u32[]{:S(2)}, u32[]{:S(2)}) collective-permute-start(s16[1040,128]{1,0:T(8,128)(2,1)S(1)} %get-tuple-element.47), channel_id=1, source_target_pairs={{0,2},{2,0},{4,6},{6,4},{8,10},{10,8},{12,14},{14,12},{16,18},{18,... | collective-permute-start | bytes 798728 | tf_op jit(solution)/shard_map/ppermute | solution.py:307
  39.4 6.0 %collective-permute-start.6 = (s16[1040,128]{1,0:T(8,128)(2,1)S(1)}, s16[1040,128]{1,0:T(8,128)(2,1)S(1)}, u32[]{:S(2)}, u32[]{:S(2)}) collective-permute-start(s16[1040,128]{1,0:T(8,128)(2,1)S(1)} %get-tuple-element.48), channel_id=1, source_target_pairs={{0,2},{2,0},{4,6},{6,4},{8,10},{10,8},{12,14},{14,12},{16,18},{18,... | collective-permute-start | bytes 798728 | tf_op jit(solution)/shard_map/ppermute | solution.py:307
